TPU v7x, 256 devices: a whole 4x4x8 slice. The times are simulated.
256 devices in a mesh: grp: 8 (over y, x_lo), curve: 32 (over z, x_hi, core).
Axes of the slice: x: 4 (x_hi: 2, x_lo: 2; x = x_hi * 2 + x_lo), y: 4, z: 8, core: 2. Of those that a mesh axis runs over, the one named last changes fastest.
Arguments:
- features: bfloat16 [1024, 8, 8, 512], P(('grp', 'curve')), may hold values from -6 to 6
- block_loads: int32 [256], P(('grp', 'curve')), may hold values from 1 to 4
- swap_counts: int32 [8, 2, 32], P('grp'), may hold values from -1 to 1, as said below
- neighbours: int32 [1024, 6], P(('grp', 'curve')), may hold values from -1 to 19, as said below
- occupancy: int32 [1024, 512], P(('grp', 'curve')), may hold values 0 or 1
- conv_weights: bfloat16 [2, 27, 64, 64], replicated, may hold values from -0.15625 to 0.15625
- norm_gains: float32 [2, 64], replicated, may hold values from 0.25 to 1.75
Outputs:
- layer_output: bfloat16 [1024, 8, 8, 512], P(('grp', 'curve'))
Inputs may be any that keep to these rules, and one draw needn't show every extreme that they name: `swap_counts`: Section-0 entries at odd owners are 0; the section-1 entry of owner 32 - 1 is 0; in each section an owner gives at most its live blocks in all, and every load stays within 0 to 4. `neighbours`: encoded as source * 4 + slot with source 0 to 4; a named slot is live after rebalancing at that source, which exists on the mesh; dead slots list -1 on every face. Of one owner's entries, at most 4 name any one of the sources 1 to 4, and some owner names exactly 4 from each of two sources.
All inputs are finite; a program needn't handle non-finite values. No bound on the sum of `occupancy` on one device may be relied on, other than what follows from the above.
Results may differ from a plain program's by a relative error of at most 0.0049.
Values may be sent and summed in bfloat16 or wider, within the bound.
A program may use at most 128 MiB of HBM per device.

v0:
```python
import jax
import jax.numpy as jnp
from jax import lax
from jax.sharding import PartitionSpec as P

OPPOSITE = (1, 0, 3, 2, 5, 4)


def extended_2(shard, sides, width):
    for axis, dim in sides:
        devices, length = (lax.axis_size(axis), shard.shape[dim])
        up = [(i, (i + 1) % devices) for i in range(devices - 1)]
        down = [(j, i) for i, j in up]
        last = lax.slice_in_dim(shard, length - width, length, axis=dim)
        leading = lax.slice_in_dim(shard, 0, width, axis=dim)
        before = lax.ppermute(last, axis, up)
        after = lax.ppermute(leading, axis, down)
        shard = jnp.concatenate([before, shard, after], axis=dim)
    return shard


def swapped(block, axis, distance):
    count = lax.axis_size(axis)
    route = []
    for low in range(count):
        high = low | 1 << distance
        if high != low and high < count:
            route += [(low, high), (high, low)]
    return lax.ppermute(block, axis, route)


def from_behind(value, axis, steps):
    count = lax.axis_size(axis)
    leading, last = (max(0, -steps), min(count, count - steps))
    return lax.ppermute(value, axis, [(source, source + steps) for source in range(leading, last)])


def face_slab(blocks, surface):
    number = blocks.shape[0]
    channels = blocks.shape[3] // 8
    if surface == 0:
        return blocks[:, 0]
    if surface == 1:
        return blocks[:, 7]
    if surface == 2:
        return blocks[:, :, 0]
    if surface == 3:
        return blocks[:, :, 7]
    layer_at = 0 if surface == 4 else 7
    cells = blocks.reshape(number, 8, 8, 8, channels)
    return cells[:, :, :, layer_at, :].reshape(number, 8, 8 * channels)


def block_faces(blocks):
    return jnp.stack([face_slab(blocks, surface) for surface in range(6)], axis=1)


def padded_block(blocks, halo_slabs):
    number = blocks.shape[0]
    channels = blocks.shape[3] // 8
    zero_column = jnp.zeros((number, 8, channels), blocks.dtype)

    def widened(slab):
        return jnp.concatenate([zero_column, slab, zero_column], axis=2)

    low_depth = halo_slabs[:, 4].reshape(number, 8, 8, channels)
    high_depth = halo_slabs[:, 5].reshape(number, 8, 8, channels)
    inner = jnp.concatenate([low_depth, blocks, high_depth], axis=3)
    inner = jnp.concatenate(
        [widened(halo_slabs[:, 2])[:, :, None], inner, widened(halo_slabs[:, 3])[:, :, None]],
        axis=2,
    )
    zero_line = jnp.zeros((number, 1, 10 * channels), blocks.dtype)
    low_plane = jnp.concatenate([zero_line, widened(halo_slabs[:, 0]), zero_line], axis=1)
    high_plane = jnp.concatenate([zero_line, widened(halo_slabs[:, 1]), zero_line], axis=1)
    return jnp.concatenate([low_plane[:, None], inner, high_plane[:, None]], axis=1)


def banded_weights(weight):
    channels = weight.shape[1]
    depth_in = jnp.arange(10)[None, :, None]
    depth_out = jnp.arange(8)[None, None, :]
    depth_shift = jnp.arange(3)[:, None, None]
    shifter = (depth_in == depth_out + depth_shift).astype(jnp.float32)
    kernel = weight.astype(jnp.float32).reshape(3, 3, 3, channels, channels)
    banded = jnp.einsum("dio,xydcq->xyicoq", shifter, kernel)
    return banded.reshape(3, 3, 10 * channels, 8 * channels).astype(jnp.bfloat16)


def convolve_banded(padded, banded):
    number = padded.shape[0]
    padded_width = padded.shape[3]
    summed = jnp.zeros((number * 64, banded.shape[3]), jnp.float32)
    for shift_y in range(3):
        strip = padded[:, :, shift_y : shift_y + 8, :]
        for shift_x in range(3):
            window = strip[:, shift_x : shift_x + 8].reshape(number * 64, padded_width)
            summed = summed + jnp.dot(
                window, banded[shift_x, shift_y], preferred_element_type=jnp.float32
            )
    return summed.reshape(number, 8, 8, banded.shape[3])


def finish_layer(summed, gain_row, keep_voxel):
    number = summed.shape[0]
    channels = gain_row.shape[0]
    voxels = summed.reshape(number, 8, 8, 8, channels)
    mean_square = jnp.mean(voxels * voxels, axis=-1, keepdims=True)
    scaled = voxels * lax.rsqrt(mean_square + 1e-05) * gain_row
    output = jnp.where(keep_voxel, jnp.maximum(scaled, 0.0), 0.0)
    return output.astype(jnp.bfloat16).reshape(number, 8, 8, 8 * channels)


def tail_blocks(blocks, filled, spare_slots):
    padding = jnp.zeros((spare_slots,) + blocks.shape[1:], blocks.dtype)
    return lax.dynamic_slice_in_dim(
        jnp.concatenate([padding, blocks], axis=0), filled, spare_slots, 0
    )


def settle_blocks(blocks, incoming, filled, swap_size, is_left):
    capacity = blocks.shape[0]
    spare_slots = incoming.shape[0]
    places = jnp.arange(capacity, dtype=jnp.int32)
    giving = jnp.maximum(swap_size, 0)
    taking = jnp.maximum(-swap_size, 0)
    left_anchor = jnp.where(
        places < filled - giving,
        places,
        jnp.where((places >= filled) & (places < filled + taking), capacity + places - filled, -1),
    )
    right_anchor = jnp.where(
        places < giving,
        capacity + spare_slots - giving + places,
        jnp.where(places < giving + filled - taking, places - giving + taking, -1),
    )
    anchor = jnp.where(is_left, left_anchor, right_anchor)
    extended = jnp.concatenate([blocks, incoming], axis=0)
    carried = jnp.take(extended, jnp.maximum(anchor, 0), axis=0)
    settled = jnp.where((anchor >= 0)[:, None, None, None], carried, jnp.zeros_like(carried))
    return (settled, jnp.where(is_left, filled - swap_size, filled + swap_size))


def settle_chain(blocks, from_below, from_above, filled, left_flow, right_flow):
    capacity = blocks.shape[0]
    spare_slots = from_below.shape[0]
    places = jnp.arange(capacity, dtype=jnp.int32)
    from_left = jnp.maximum(left_flow, 0)
    to_left = jnp.maximum(-left_flow, 0)
    to_right = jnp.maximum(right_flow, 0)
    from_right = jnp.maximum(-right_flow, 0)
    middle = filled - to_left - to_right
    anchor = jnp.where(
        places < from_left,
        capacity + spare_slots - from_left + places,
        jnp.where(
            places < from_left + middle,
            places - from_left + to_left,
            jnp.where(
                places < from_left + middle + from_right,
                capacity + spare_slots + places - from_left - middle,
                -1,
            ),
        ),
    )
    extended = jnp.concatenate([blocks, from_below, from_above], axis=0)
    carried = jnp.take(extended, jnp.maximum(anchor, 0), axis=0)
    settled = jnp.where((anchor >= 0)[:, None, None, None], carried, jnp.zeros_like(carried))
    return (settled, filled + left_flow - right_flow)


def surface_sources(payload):
    along_curve = extended_2(payload[None], (("curve", 0),), 1)
    across_groups = extended_2(payload[None], (("grp", 0),), 1)
    return (payload, along_curve[0], along_curve[2], across_groups[0], across_groups[2])


def local(features, block_loads, swap_counts, neighbours, occupancy, conv_weights, norm_gains):
    capacity = features.shape[0]
    channels = features.shape[3] // 8
    spare_slots = capacity // 4
    owner_here = lax.axis_index("curve")
    owners = lax.axis_size("curve")
    filled = block_loads[0]
    blocks = features
    is_left = owner_here % 2 == 0
    swap_size = swap_counts[0, 0, owner_here - owner_here % 2]
    outgoing = jnp.where(is_left, tail_blocks(blocks, filled, spare_slots), blocks[:spare_slots])
    incoming = swapped(outgoing, "curve", 0)
    blocks, filled = settle_blocks(blocks, incoming, filled, swap_size, is_left)
    left_flow = jnp.where(owner_here > 0, swap_counts[0, 1, jnp.maximum(owner_here - 1, 0)], 0)
    right_flow = jnp.where(owner_here < owners - 1, swap_counts[0, 1, owner_here], 0)
    from_below = from_behind(tail_blocks(blocks, filled, spare_slots), "curve", 1)
    from_above = from_behind(blocks[:spare_slots], "curve", -1)
    blocks, filled = settle_chain(blocks, from_below, from_above, filled, left_flow, right_flow)
    is_live = jnp.arange(capacity) < filled
    keep_voxel = (is_live[:, None] & (occupancy > 0)).reshape(capacity, 8, 8, 8, 1)
    values = jnp.where(
        keep_voxel, blocks.reshape(capacity, 8, 8, 8, channels), jnp.zeros((), blocks.dtype)
    ).reshape(blocks.shape)
    source = jnp.where(neighbours >= 0, neighbours // capacity, -1)
    within = neighbours % capacity
    opposite = jnp.array(OPPOSITE, jnp.int32)[None, :]
    lookup = (within * 6 + opposite).reshape(-1)
    for layer_no in range(conv_weights.shape[0]):
        all_faces = block_faces(values)
        flat_faces = all_faces.reshape(capacity * 6, 8, 8 * channels)
        own_picked = jnp.take(flat_faces, lookup, axis=0).reshape(capacity, 6, 8, 8 * channels)
        halo_slabs = jnp.where(
            (source == 0)[:, :, None, None], own_picked, jnp.zeros_like(own_picked)
        )
        sources = surface_sources(all_faces)
        for source_no in range(1, 5):
            remote_faces = sources[source_no].reshape(capacity * 6, 8, 8 * channels)
            picked = jnp.take(remote_faces, lookup, axis=0).reshape(capacity, 6, 8, 8 * channels)
            halo_slabs = jnp.where((source == source_no)[:, :, None, None], picked, halo_slabs)
        padded = padded_block(values, halo_slabs)
        summed = convolve_banded(padded, banded_weights(conv_weights[layer_no]))
        values = finish_layer(summed, norm_gains[layer_no], keep_voxel)
    return values


def solution(mesh):
    return jax.shard_map(
        local,
        mesh=mesh,
        in_specs=(
            P(("grp", "curve"), None, None, None),
            P(("grp", "curve")),
            P("grp", None, None),
            P(("grp", "curve"), None),
            P(("grp", "curve"), None),
            P(),
            P(),
        ),
        out_specs=P(("grp", "curve"), None, None, None),
        check_vma=False,
    )
```

profile of v0, /device:TPU:119, one launch (start us, length us, event | category | flops | bytes accessed | tf_op | source)
XLA Modules:
  0.0 203.7 jit_solution(6409381479003276534)
XLA Ops:
  2.3 1.4 constant_dynamic-slice_fusion
  12.1 1.2 fusion.49
  13.3 6.3 %convert_bitcast_fusion.1 = bf16[3,3,10,64,8,64]{5,2,3,1,0,4:T(8,128)(2,1)S(1)} fusion(bf16[3,3,3,64,64]{4,3,2,1,0:T(8,128)(2,1)S(1)} %bitcast.290, s32[3,8]{0,1:T(8,128)S(1)} %iota_add_fusion), kind=kOutput, calls=%fused_computation.13 | convolution fusion | flops 20644080 | bytes 6119520 | tf_op jit(solution)/shard_map/dio,xydcq->xyicoq/dot_general | solution.py:86
  19.6 22.2 %copy.193 = bf16[3,3,10,64,8,64]{5,4,3,2,1,0:T(8,128)(2,1)} copy(bf16[3,3,10,64,8,64]{5,2,3,1,0,4:T(8,128)(2,1)S(1)} %convert_bitcast_fusion.1) | data formatting | bytes 11796480 | tf_op jit(solution)/shard_map/convert_element_type | solution.py:87
  41.8 16.3 %convert_element_type.37 = bf16[3,3,640,512]{3,2,1,0:T(8,128)(2,1)} reshape(bf16[3,3,10,64,8,64]{5,4,3,2,1,0:T(8,128)(2,1)} %copy.193) | data formatting | bytes 11796480 | tf_op jit(solution)/shard_map/convert_element_type | solution.py:87
  58.6 6.1 %convert_bitcast_fusion = bf16[3,3,10,64,8,64]{5,2,3,1,0,4:T(8,128)(2,1)S(1)} fusion(bf16[3,3,3,64,64]{4,3,2,1,0:T(8,128)(2,1)S(1)} %bitcast.289, s32[3,8]{0,1:T(8,128)S(1)} %iota_add_fusion), kind=kOutput, calls=%fused_computation.12 | convolution fusion | flops 20644080 | bytes 6119520 | tf_op jit(solution)/shard_map/dio,xydcq->xyicoq/dot_general | solution.py:86
  64.7 22.2 %copy.213 = bf16[3,3,10,64,8,64]{5,4,3,2,1,0:T(8,128)(2,1)} copy(bf16[3,3,10,64,8,64]{5,2,3,1,0,4:T(8,128)(2,1)S(1)} %convert_bitcast_fusion) | data formatting | bytes 11796480 | tf_op jit(solution)/shard_map/convert_element_type | solution.py:87
  86.9 16.4 %convert_element_type.42 = bf16[3,3,640,512]{3,2,1,0:T(8,128)(2,1)} reshape(bf16[3,3,10,64,8,64]{5,4,3,2,1,0:T(8,128)(2,1)} %copy.213) | data formatting | bytes 11796480 | tf_op jit(solution)/shard_map/convert_element_type | solution.py:87
  104.7 5.5 %collective-permute-start.1 = (bf16[1,8,8,512]{3,2,1,0:T(8,128)(2,1)S(1)}, bf16[1,8,8,512]{3,2,1,0:T(8,128)(2,1)S(1)}, u32[]{:S(2)}, u32[]{:S(2)}) collective-permute-start(bf16[1,8,8,512]{3,2,1,0:T(8,128)(2,1)S(1)} %get-tuple-element.42), channel_id=1, source_target_pairs={{0,1},{1,2},{2,3},{3,4},{4,5},{5,6},{6,7},{7,8},{8,9},{9,10},{10,1... | collective-permute-start | bytes 196616 | tf_op jit(solution)/shard_map/ppermute | solution.py:35
  110.3 1.9 collective-permute-start.2
  112.2 7.2 %collective-permute-done.2 = bf16[1,8,8,512]{3,2,1,0:T(8,128)(2,1)S(1)} collective-permute-done((bf16[1,8,8,512]{3,2,1,0:T(8,128)(2,1)S(1)}, bf16[1,8,8,512]{3,2,1,0:T(8,128)(2,1)S(1)}, u32[]{:S(2)}, u32[]{:S(2)}) %collective-permute-start.2) | collective-permute-done | bytes 65568 | tf_op jit(solution)/shard_map/ppermute | solution.py:35
  125.1 1.9 collective-permute-start.3
  127.0 4.3 %collective-permute-start.4 = (bf16[1,4,6,8,512]{4,3,2,1,0:T(8,128)(2,1)}, bf16[1,4,6,8,512]{4,3,2,1,0:T(8,128)(2,1)S(1)}, u32[]{:S(2)}, u32[]{:S(2)}) collective-permute-start(bf16[1,4,6,8,512]{4,3,2,1,0:T(8,128)(2,1)} %bitcast.10), channel_id=1, source_target_pairs={{0,32},{32,64},{64,96},{96,128},{128,160},{160,192},{192,224},{1,3... | collective-permute-start | bytes 589832 | tf_op jit(solution)/shard_map/ppermute | solution.py:16
  131.2 1.9 collective-permute-start.5
  133.2 7.3 %collective-permute-start.6 = (bf16[1,4,6,8,512]{4,3,2,1,0:T(8,128)(2,1)}, bf16[1,4,6,8,512]{4,3,2,1,0:T(8,128)(2,1)}, u32[]{:S(2)}, u32[]{:S(2)}) collective-permute-start(bf16[1,4,6,8,512]{4,3,2,1,0:T(8,128)(2,1)} %bitcast.10), channel_id=1, source_target_pairs={{0,1},{1,2},{2,3},{3,4},{4,5},{5,6},{6,7},{7,8},{8,9},{9,10},{10,1... | collective-permute-start | bytes 589832 | tf_op jit(solution)/shard_map/ppermute | solution.py:16
  140.4 1.5 gather_fusion.6
  142.1 1.5 gather_fusion.2
  144.3 1.5 gather_fusion.3
  146.5 1.5 gather_fusion.4
  148.0 2.2 %gather_fusion.5 = bf16[24,8,512]{2,1,0:T(8,128)(2,1)} fusion(bf16[24,8,512]{2,1,0:T(8,128)(2,1)} %bitcast.17, s32[1024]{0:T(1024)S(1)} %pad_clamp_fusion), kind=kCustom, calls=%fused_computation.3.clone | custom fusion | bytes 393312 | tf_op jit(solution)/shard_map/jit(_take)/gather | solution.py:215
  161.0 1.2 select_convert_fusion.2
  162.9 1.4 fusion.3
  167.7 1.9 collective-permute-start.7
  169.6 4.3 %collective-permute-start.8 = (bf16[1,4,6,8,512]{4,3,2,1,0:T(8,128)(2,1)}, bf16[1,4,6,8,512]{4,3,2,1,0:T(8,128)(2,1)}, u32[]{:S(2)}, u32[]{:S(2)}) collective-permute-start(bf16[1,4,6,8,512]{4,3,2,1,0:T(8,128)(2,1)} %bitcast.319), channel_id=1, source_target_pairs={{0,32},{32,64},{64,96},{96,128},{128,160},{160,192},{192,224},{1,3... | collective-permute-start | bytes 589832 | tf_op jit(solution)/shard_map/ppermute | solution.py:16
  173.9 1.9 collective-permute-start.9
  175.8 7.5 %collective-permute-start.10 = (bf16[1,4,6,8,512]{4,3,2,1,0:T(8,128)(2,1)}, bf16[1,4,6,8,512]{4,3,2,1,0:T(8,128)(2,1)}, u32[]{:S(2)}, u32[]{:S(2)}) collective-permute-start(bf16[1,4,6,8,512]{4,3,2,1,0:T(8,128)(2,1)} %bitcast.321), channel_id=1, source_target_pairs={{0,1},{1,2},{2,3},{3,4},{4,5},{5,6},{6,7},{7,8},{8,9},{9,10},{10,1... | collective-permute-start | bytes 589832 | tf_op jit(solution)/shard_map/ppermute | solution.py:16
  183.4 2.2 %gather_fusion.11 = bf16[24,8,512]{2,1,0:T(8,128)(2,1)} fusion(bf16[24,8,512]{2,1,0:T(8,128)(2,1)} %bitcast.322, s32[1024]{0:T(1024)S(1)} %pad_clamp_fusion), kind=kCustom, calls=%fused_computation.9.clone | custom fusion | bytes 393312 | tf_op jit(solution)/shard_map/jit(_take)/gather | solution.py:208
  186.4 1.5 gather_fusion.7
  187.9 1.5 gather_fusion.8
  189.4 1.5 gather_fusion.9
  190.9 1.5 gather_fusion.10
  192.4 1.1 broadcast_select_fusion
  (183 shorter events, 40.3 us)
Async XLA Ops:
  1.6 102.4 %collective-permute-start = (bf16[1,8,8,512]{3,2,1,0:T(8,128)(2,1)S(1)}, bf16[1,8,8,512]{3,2,1,0:T(8,128)(2,1)S(1)}, u32[]{:S(2)}, u32[]{:S(2)}) collective-permute-start(bf16[1,8,8,512]{3,2,1,0:T(8,128)(2,1)S(1)} %fusion.28), channel_id=1, source_target_pairs={{0,1},{1,0},{2,3},{3,2},{4,5},{5,4},{6,7},{7,6},{8,9},{9,8},{10,11... | collective-permute-start | bytes 196616 | tf_op jit(solution)/shard_map/ppermute | solution.py:29
  8.5 141.7 %copy-start.14 = (pred[24]{0:T(512)(128)(4,1)}, pred[24]{0:T(512)(128)(4,1)S(1)}, u32[]{:S(2)}) copy-start(pred[24]{0:T(512)(128)(4,1)S(1)} %compare_and_fusion.1) | copy-start | bytes 76
  10.3 110.9 %copy-start.2 = (pred[4,8,8,8]{2,1,0,3:T(8,128)(4,1)}, pred[4,8,8,8]{2,1,0,3:T(8,128)(4,1)S(1)}, u32[]{:S(2)}) copy-start(pred[4,8,8,8]{2,1,0,3:T(8,128)(4,1)S(1)} %copy.172) | copy-start | bytes 6148
  11.6 139.6 %copy-start.9 = (pred[4,6]{0,1:T(8,128)(4,1)}, pred[4,6]{0,1:T(8,128)(4,1)S(1)}, u32[]{:S(2)}) copy-start(pred[4,6]{0,1:T(8,128)(4,1)S(1)} %copy.180) | copy-start | bytes 76
  11.7 139.5 %copy-start.10 = (pred[4,6]{0,1:T(8,128)(4,1)}, pred[4,6]{0,1:T(8,128)(4,1)S(1)}, u32[]{:S(2)}) copy-start(pred[4,6]{0,1:T(8,128)(4,1)S(1)} %copy.181) | copy-start | bytes 76
  11.8 139.4 %copy-start.11 = (pred[4,6]{0,1:T(8,128)(4,1)}, pred[4,6]{0,1:T(8,128)(4,1)S(1)}, u32[]{:S(2)}) copy-start(pred[4,6]{0,1:T(8,128)(4,1)S(1)} %copy.182) | copy-start | bytes 76
  12.0 139.3 %copy-start.12 = (pred[4,6]{0,1:T(8,128)(4,1)}, pred[4,6]{0,1:T(8,128)(4,1)S(1)}, u32[]{:S(2)}) copy-start(pred[4,6]{0,1:T(8,128)(4,1)S(1)} %copy.183) | copy-start | bytes 76
  12.1 139.2 %copy-start.13 = (pred[4,6]{0,1:T(8,128)(4,1)}, pred[4,6]{0,1:T(8,128)(4,1)S(1)}, u32[]{:S(2)}) copy-start(pred[4,6]{0,1:T(8,128)(4,1)S(1)} %copy.174) | copy-start | bytes 76
  41.8 16.7 %copy-start.15 = (f32[2,64]{1,0:T(2,128)S(1)}, f32[2,64]{1,0:T(2,128)}, u32[]{:S(2)}) copy-start(f32[2,64]{1,0:T(2,128)} %param.16) | copy-start | bytes 1540
  58.5 6.2 %copy-start.8 = (f32[64]{0:T(128)}, f32[64]{0:T(128)S(1)}, u32[]{:S(2)}) copy-start(f32[64]{0:T(128)S(1)} %get-tuple-element.69) | copy-start | bytes 772
  86.9 17.1 %copy-start = (bf16[4,8,8,512]{3,2,1,0:T(8,128)(2,1)S(1)}, bf16[4,8,8,512]{3,2,1,0:T(8,128)(2,1)}, u32[]{:S(2)}) copy-start(bf16[4,8,8,512]{3,2,1,0:T(8,128)(2,1)} %param.10) | copy-start | bytes 786436
  104.7 7.5 %collective-permute-start.1 = (bf16[1,8,8,512]{3,2,1,0:T(8,128)(2,1)S(1)}, bf16[1,8,8,512]{3,2,1,0:T(8,128)(2,1)S(1)}, u32[]{:S(2)}, u32[]{:S(2)}) collective-permute-start(bf16[1,8,8,512]{3,2,1,0:T(8,128)(2,1)S(1)} %get-tuple-element.42), channel_id=1, source_target_pairs={{0,1},{1,2},{2,3},{3,4},{4,5},{5,6},{6,7},{7,8},{8,9},{9,10},{10,1... | collective-permute-start | bytes 196616 | tf_op jit(solution)/shard_map/ppermute | solution.py:35
  110.3 9.2 %collective-permute-start.2 = (bf16[1,8,8,512]{3,2,1,0:T(8,128)(2,1)S(1)}, bf16[1,8,8,512]{3,2,1,0:T(8,128)(2,1)S(1)}, u32[]{:S(2)}, u32[]{:S(2)}) collective-permute-start(bf16[1,8,8,512]{3,2,1,0:T(8,128)(2,1)S(1)} %get-tuple-element.43), channel_id=1, source_target_pairs={{1,0},{2,1},{3,2},{4,3},{5,4},{6,5},{7,6},{8,7},{9,8},{10,9},{11,1... | collective-permute-start | bytes 196616 | tf_op jit(solution)/shard_map/ppermute | solution.py:35
  123.8 31.3 %slice-start.2 = ((s8[5898240]{0:T(1024)(128)(4,1)}), s8[1703936]{0:T(1024)(128)(4,1)S(1)}, s32[]{:S(2)}) async-start(s8[5898240]{0:T(1024)(128)(4,1)} %bitcast.286), calls=%async_computation.2 | async-start | bytes 3407872
  125.1 17.0 %collective-permute-start.3 = (bf16[1,4,6,8,512]{4,3,2,1,0:T(8,128)(2,1)}, bf16[1,4,6,8,512]{4,3,2,1,0:T(8,128)(2,1)}, u32[]{:S(2)}, u32[]{:S(2)}) collective-permute-start(bf16[1,4,6,8,512]{4,3,2,1,0:T(8,128)(2,1)} %bitcast.10), channel_id=1, source_target_pairs={{32,0},{64,32},{96,64},{128,96},{160,128},{192,160},{224,192},{33,... | collective-permute-start | bytes 589832 | tf_op jit(solution)/shard_map/ppermute | solution.py:17
  127.0 16.6 %collective-permute-start.4 = (bf16[1,4,6,8,512]{4,3,2,1,0:T(8,128)(2,1)}, bf16[1,4,6,8,512]{4,3,2,1,0:T(8,128)(2,1)S(1)}, u32[]{:S(2)}, u32[]{:S(2)}) collective-permute-start(bf16[1,4,6,8,512]{4,3,2,1,0:T(8,128)(2,1)} %bitcast.10), channel_id=1, source_target_pairs={{0,32},{32,64},{64,96},{96,128},{128,160},{160,192},{192,224},{1,3... | collective-permute-start | bytes 589832 | tf_op jit(solution)/shard_map/ppermute | solution.py:16
  131.2 14.5 %collective-permute-start.5 = (bf16[1,4,6,8,512]{4,3,2,1,0:T(8,128)(2,1)}, bf16[1,4,6,8,512]{4,3,2,1,0:T(8,128)(2,1)S(1)}, u32[]{:S(2)}, u32[]{:S(2)}) collective-permute-start(bf16[1,4,6,8,512]{4,3,2,1,0:T(8,128)(2,1)} %bitcast.10), channel_id=1, source_target_pairs={{1,0},{2,1},{3,2},{4,3},{5,4},{6,5},{7,6},{8,7},{9,8},{10,9},{11,1... | collective-permute-start | bytes 589832 | tf_op jit(solution)/shard_map/ppermute | solution.py:17
  133.2 14.8 %collective-permute-start.6 = (bf16[1,4,6,8,512]{4,3,2,1,0:T(8,128)(2,1)}, bf16[1,4,6,8,512]{4,3,2,1,0:T(8,128)(2,1)}, u32[]{:S(2)}, u32[]{:S(2)}) collective-permute-start(bf16[1,4,6,8,512]{4,3,2,1,0:T(8,128)(2,1)} %bitcast.10), channel_id=1, source_target_pairs={{0,1},{1,2},{2,3},{3,4},{4,5},{5,6},{6,7},{7,8},{8,9},{9,10},{10,1... | collective-permute-start | bytes 589832 | tf_op jit(solution)/shard_map/ppermute | solution.py:16
  143.6 0.7 copy-start.5
  145.8 0.7 copy-start.4
  152.8 1.9 copy-start.6
  152.8 2.3 %slice-start.3 = ((s8[5898240]{0:T(1024)(128)(4,1)}), s8[4194304]{0:T(1024)(128)(4,1)S(1)}, s32[]{:S(2)}) async-start(s8[5898240]{0:T(1024)(128)(4,1)} %bitcast.286), calls=%async_computation.3 | async-start | bytes 8388608
  154.7 1.9 copy-start.3
  167.7 18.7 %collective-permute-start.7 = (bf16[1,4,6,8,512]{4,3,2,1,0:T(8,128)(2,1)}, bf16[1,4,6,8,512]{4,3,2,1,0:T(8,128)(2,1)}, u32[]{:S(2)}, u32[]{:S(2)}) collective-permute-start(bf16[1,4,6,8,512]{4,3,2,1,0:T(8,128)(2,1)} %bitcast.318), channel_id=1, source_target_pairs={{32,0},{64,32},{96,64},{128,96},{160,128},{192,160},{224,192},{33,... | collective-permute-start | bytes 589832 | tf_op jit(solution)/shard_map/ppermute | solution.py:17
  169.6 18.2 %collective-permute-start.8 = (bf16[1,4,6,8,512]{4,3,2,1,0:T(8,128)(2,1)}, bf16[1,4,6,8,512]{4,3,2,1,0:T(8,128)(2,1)}, u32[]{:S(2)}, u32[]{:S(2)}) collective-permute-start(bf16[1,4,6,8,512]{4,3,2,1,0:T(8,128)(2,1)} %bitcast.319), channel_id=1, source_target_pairs={{0,32},{32,64},{64,96},{96,128},{128,160},{160,192},{192,224},{1,3... | collective-permute-start | bytes 589832 | tf_op jit(solution)/shard_map/ppermute | solution.py:16
  173.9 15.5 %collective-permute-start.9 = (bf16[1,4,6,8,512]{4,3,2,1,0:T(8,128)(2,1)}, bf16[1,4,6,8,512]{4,3,2,1,0:T(8,128)(2,1)}, u32[]{:S(2)}, u32[]{:S(2)}) collective-permute-start(bf16[1,4,6,8,512]{4,3,2,1,0:T(8,128)(2,1)} %bitcast.320), channel_id=1, source_target_pairs={{1,0},{2,1},{3,2},{4,3},{5,4},{6,5},{7,6},{8,7},{9,8},{10,9},{11,1... | collective-permute-start | bytes 589832 | tf_op jit(solution)/shard_map/ppermute | solution.py:17
  175.8 15.1 %collective-permute-start.10 = (bf16[1,4,6,8,512]{4,3,2,1,0:T(8,128)(2,1)}, bf16[1,4,6,8,512]{4,3,2,1,0:T(8,128)(2,1)}, u32[]{:S(2)}, u32[]{:S(2)}) collective-permute-start(bf16[1,4,6,8,512]{4,3,2,1,0:T(8,128)(2,1)} %bitcast.321), channel_id=1, source_target_pairs={{0,1},{1,2},{2,3},{3,4},{4,5},{5,6},{6,7},{7,8},{8,9},{9,10},{10,1... | collective-permute-start | bytes 589832 | tf_op jit(solution)/shard_map/ppermute | solution.py:16
  185.5 12.7 %slice-start = ((s8[5898240]{0:T(1024)(128)(4,1)}), s8[1703936]{0:T(1024)(128)(4,1)S(1)}, s32[]{:S(2)}) async-start(s8[5898240]{0:T(1024)(128)(4,1)} %bitcast.284), calls=%async_computation | async-start | bytes 3407872
  195.1 3.1 %slice-start.1 = ((s8[5898240]{0:T(1024)(128)(4,1)}), s8[4194304]{0:T(1024)(128)(4,1)S(1)}, s32[]{:S(2)}) async-start(s8[5898240]{0:T(1024)(128)(4,1)} %bitcast.284), calls=%async_computation.1 | async-start | bytes 8388608
  197.8 1.9 copy-start.1
  200.5 2.3 %copy-start.7 = (f32[512]{0:T(512)S(1)}, f32[512]{0:T(512)}, u32[]{:S(2)}) copy-start(f32[512]{0:T(512)} %mul.104) | copy-start | bytes 6148
where the time goes:
time: 206 us; the launch traced here: 204 us
  local copies, waits for them, and re-layouts  115 us (56%)
  starting transfers between devices  39.2 us (19%)
  matrix products  19.2 us (9%)
  other arithmetic  17.1 us (8%)
  waiting for transfers between devices  7.27 us (4%)
  between operations  5.65 us (3%)
    convert_element_type x4, local copies, waits for them, and re-layouts, banded_weights(): banded.reshape(3, 3, 10 * channels, 8 * channels).astype(jnp.bfloat16)  77.1 us
    ppermute x4, starting transfers between devices, extended_2(): before = lax.ppermute(last, axis, up)  23.3 us
    gather x8, local copies, waits for them, and re-layouts, local(): jnp.take(remote_faces, lookup, axis=0).reshape(capacity, 6, 8, 8 * channels)  12.6 us
    dot_general x2, matrix products, banded_weights(): banded = jnp.einsum('dio,xydcq->xyicoq', shifter, kernel)  12.5 us
    ppermute x4, starting transfers between devices, extended_2(): after = lax.ppermute(leading, axis, down)  7.66 us
    unnamed x50, local copies, waits for them, and re-layouts  7.61 us
    ppermute x2, starting transfers between devices, from_behind(): lax.ppermute(value, axis, [(source, source + steps) for source in range(l...  7.44 us
    ppermute x2, waiting for transfers between devices, from_behind(): lax.ppermute(value, axis, [(source, source + steps) for source in range(l...  7.25 us
  transfers between devices with their start and end apart: 11, of which 1 were waited for; matrix products, arithmetic and copies ran while one was open for 55% of the time, Pallas kernels for 0%

commit v1 on v0

v1 whole, which is shorter than its diff:
```python
import functools

import jax
import jax.numpy as jnp
from jax import lax
from jax.experimental import pallas as pl
from jax.experimental.pallas import tpu as pltpu
from jax.sharding import PartitionSpec as P

F32 = jnp.float32
BF16 = jnp.bfloat16
I32 = jnp.int32
MESH = pl.DeviceIdType.MESH


def lanes_low():
    return lax.broadcasted_iota(I32, (8, 128), 1) < 64


def half_turn(tile):
    return pltpu.roll(tile, 64, 1)


def widen(tiles, low_side, high_side):
    low = lanes_low()
    turned = [half_turn(t) for t in tiles]
    out = [jnp.where(low, low_side, turned[0])]
    for t in range(1, 4):
        out.append(jnp.where(low, turned[t - 1], turned[t]))
    out.append(jnp.where(low, turned[3], high_side))
    return jnp.concatenate(out, axis=1)


def kernel(
    groups,
    owners,
    feat,
    loads,
    swaps,
    nbrs,
    occ,
    wts,
    gains,
    out,
    blocks,
    moved,
    outgoing,
    loads_s,
    swaps_s,
    nbrs_s,
    asked_s,
    own_at,
    far_at,
    kind_at,
    occ_v,
    w_v,
    g_v,
    banded,
    mask,
    nat,
    faces,
    send_f,
    recv_first,
    recv_second,
    lhs,
    y_rows,
    in_sems,
    list_send,
    list_recv,
    block_send,
    block_recv,
    face_send,
    face_recv,
):
    grp = lax.axis_index("grp")
    own = lax.axis_index("curve")
    odd = lax.rem(own, 2) == 1
    before = (grp, lax.rem(own + owners - 1, owners))
    after = (grp, lax.rem(own + 1, owners))
    below = (lax.rem(grp + groups - 1, groups), own)
    above = (lax.rem(grp + 1, groups), own)
    sides = (before, after, below, above)

    local = [
        pltpu.make_async_copy(feat, blocks, in_sems.at[0]),
        pltpu.make_async_copy(loads, loads_s, in_sems.at[1]),
        pltpu.make_async_copy(swaps, swaps_s, in_sems.at[2]),
        pltpu.make_async_copy(nbrs, nbrs_s, in_sems.at[3]),
        pltpu.make_async_copy(occ, occ_v, in_sems.at[4]),
        pltpu.make_async_copy(wts, w_v, in_sems.at[5]),
        pltpu.make_async_copy(gains, g_v, in_sems.at[6]),
    ]
    for copy in local:
        copy.start()

    barrier = pltpu.get_barrier_semaphore()
    for device in sides:
        pl.semaphore_signal(barrier, inc=1, device_id=device, device_id_type=MESH)
    pl.semaphore_wait(barrier, 4)

    lists = [
        pltpu.make_async_remote_copy(
            src_ref=nbrs,
            dst_ref=asked_s.at[i ^ 1],
            send_sem=list_send.at[i],
            recv_sem=list_recv.at[i ^ 1],
            device_id=sides[i],
            device_id_type=MESH,
        )
        for i in range(4)
    ]
    for copy in lists:
        copy.start()

    local[1].wait()
    local[0].wait()
    load = loads_s[0]
    tail = jnp.maximum(load - 1, 0)
    outgoing[2] = blocks[jnp.where(odd, tail, 0)]
    partner = (grp, own + 1 - 2 * lax.rem(own, 2))
    across = (grp, lax.rem(own + owners - 1 + 2 * lax.rem(own, 2), owners))
    cross_copy = pltpu.make_async_remote_copy(
        src_ref=outgoing.at[pl.ds(2, 1)],
        dst_ref=moved.at[pl.ds(2, 1)],
        send_sem=block_send.at[0],
        recv_sem=block_recv.at[0],
        device_id=across,
        device_id_type=MESH,
    )
    cross_copy.start()
    outgoing[0] = blocks[jnp.where(odd, 0, jnp.maximum(load - 2, 0))]
    outgoing[1] = blocks[jnp.where(odd, 1, tail)]
    pair_copy = pltpu.make_async_remote_copy(
        src_ref=outgoing.at[pl.ds(0, 2)],
        dst_ref=moved.at[pl.ds(0, 2)],
        send_sem=block_send.at[1],
        recv_sem=block_recv.at[1],
        device_id=partner,
        device_id_type=MESH,
    )
    pair_copy.start()

    for copy in local[2:]:
        copy.wait()

    zero_w = jnp.zeros((64, 64), BF16)
    for layer in range(2):
        for dx in range(3):
            for dy in range(3):
                w = [w_v[layer, dx * 9 + dy * 3 + dz] for dz in range(3)]
                rows = [(w[0], zero_w), (w[1], w[0]), (w[2], w[1]), (zero_w, w[2])]
                for zi in range(4):
                    banded[layer, pl.ds((dy * 4 + zi) * 64, 64), pl.ds(dx * 128, 128)] = (
                        jnp.concatenate(rows[zi], axis=1)
                    )

    swap = swaps_s[0, 0, own - lax.rem(own, 2)]
    flow_in = jnp.where(own > 0, swaps_s[0, 1, jnp.maximum(own - 1, 0)], 0)
    flow_out = jnp.where(own < owners - 1, swaps_s[0, 1, own], 0)
    first_load = load + jnp.where(odd, swap, -swap)
    came = jnp.maximum(flow_in, 0)
    dropped = jnp.maximum(-flow_in, 0)
    middle = first_load - dropped - jnp.maximum(flow_out, 0)
    taken = jnp.maximum(-flow_out, 0)
    final = first_load + flow_in - flow_out
    came_at = jnp.where(odd, jnp.where(swap > 0, 4, jnp.where(swap < 0, 0, 5)), 6)
    taken_at = jnp.where(odd, 6, jnp.where(swap > 0, tail, jnp.where(swap < 0, 5, 4)))
    places = []
    for j in range(4):
        i = j - came + dropped
        even_at = jnp.where(i < load - jnp.maximum(swap, 0), i, 4)
        odd_at = jnp.where((swap > 0) & (i == 0), 5, i - swap)
        kept_at = jnp.where(odd, odd_at, even_at)
        at = jnp.where(
            j < came,
            came_at,
            jnp.where(j < came + middle, kept_at, jnp.where(j < came + middle + taken, taken_at, 0)),
        )
        places.append(jnp.clip(at, 0, 6))

    block_no = lax.broadcasted_iota(I32, (4, 512), 0)
    occupied = jnp.where((block_no < final) & (occ_v[...] > 0), 1.0, 0.0).astype(F32)
    lane3 = lax.broadcasted_iota(I32, (4, 8, 128), 2)
    sub3 = lax.broadcasted_iota(I32, (4, 8, 128), 1)
    strips = []
    for x in range(8):
        strip = occupied[:, 128 * (x // 2) : 128 * (x // 2) + 128]
        wide = jnp.broadcast_to(strip[:, None, :], (4, 8, 128))
        pick = (lane3 // 8) == (sub3 + 8 * (x % 2))
        strips.append(jnp.where(pick, wide, 0.0).reshape(32, 128))
    strips = jnp.concatenate(strips, axis=0).astype(BF16)
    spread = jnp.where(
        lax.rem(lax.broadcasted_iota(I32, (128, 512), 0), 8)
        == lax.broadcasted_iota(I32, (128, 512), 1) // 64,
        1.0,
        0.0,
    ).astype(BF16)
    mask[...] = jnp.dot(strips, spread, preferred_element_type=F32)

    def rank_step(b, counts):
        counts = list(counts)
        for f in range(6):
            v = nbrs_s[b, f]
            s = lax.shift_right_arithmetic(v, 2)
            rank = jnp.int32(0)
            for i in range(4):
                hit = s == i + 1
                rank = jnp.where(hit, 4 * i + counts[i], rank)
                counts[i] = counts[i] + hit.astype(I32)
            kind_at[b, f] = s
            own_at[b, f] = jnp.where(v >= 0, (v & 3) * 6 + (f ^ 1), 0)
            far_at[b, f] = jnp.clip(rank, 0, 15)
        return tuple(counts)

    lax.fori_loop(0, 4, rank_step, (jnp.int32(0),) * 4)

    for copy in lists:
        copy.wait_recv()

    def ask_step(b, state):
        state = [list(row) for row in state]
        for f in range(6):
            for i in range(4):
                v = asked_s[i, b, f]
                count = state[i][4]
                hit = lax.shift_right_arithmetic(v, 2) == (i ^ 1) + 1
                face = (v & 3) * 6 + (f ^ 1)
                for j in range(4):
                    state[i][j] = jnp.where(hit & (count == j), face, state[i][j])
                state[i][4] = count + hit.astype(I32)
        return tuple(tuple(row) for row in state)

    asked = lax.fori_loop(0, 4, ask_step, ((jnp.int32(0),) * 5,) * 4)

    cross_copy.wait_recv()
    pair_copy.wait_recv()
    for j in range(4):
        mine = blocks[jnp.minimum(places[j], 3)].astype(F32)
        other = moved[jnp.maximum(places[j] - 4, 0)].astype(F32)
        block = jnp.where(places[j] < 4, mine, other)
        for x in range(8):
            rows = pl.ds(x * 32 + j * 8, 8)
            kept = jnp.where(mask[rows, :] > 0.5, block[8 * x : 8 * x + 8], 0.0)
            for t in range(4):
                nat[t, rows, :] = kept[:, 128 * t : 128 * t + 128]

    low = lanes_low()
    sub = lax.broadcasted_iota(I32, (8, 640), 0)
    none8 = jnp.zeros((8, 128), F32)
    group_lane = lax.broadcasted_iota(I32, (256, 128), 1) // 64
    group_row = lax.rem(lax.broadcasted_iota(I32, (256, 128), 0), 128) // 64
    averager = jnp.where(group_lane == group_row, 1.0 / 64.0, 0.0).astype(BF16)

    for layer in range(2):
        recv_f = (recv_first, recv_second)[layer]
        for b in range(4):
            for f in range(2):
                r = 7 * f * 32 + b * 8
                face = [nat[t, pl.ds(r, 8), :] for t in range(4)]
                faces[b * 6 + f] = jnp.concatenate(face, axis=0).astype(BF16)
                face = [
                    nat[t, pl.ds(b * 8 + 7 * f, 8, stride=32), :] for t in range(4)
                ]
                faces[b * 6 + 2 + f] = jnp.concatenate(face, axis=0).astype(BF16)
            face = []
            for x in range(4):
                here = nat[0, pl.ds(x * 32 + b * 8, 8), :]
                there = nat[0, pl.ds((x + 4) * 32 + b * 8, 8), :]
                face.append(jnp.where(low, here, half_turn(there)))
            faces[b * 6 + 4] = jnp.concatenate(face, axis=0).astype(BF16)
            face = []
            for x in range(4):
                here = nat[3, pl.ds(x * 32 + b * 8, 8), :]
                there = nat[3, pl.ds((x + 4) * 32 + b * 8, 8), :]
                face.append(jnp.where(low, half_turn(here), there))
            faces[b * 6 + 5] = jnp.concatenate(face, axis=0).astype(BF16)
        copies = []
        for i in range(4):
            for j in range(4):
                send_f[layer, 4 * i + j] = faces[asked[i][j]]
            copy = pltpu.make_async_remote_copy(
                src_ref=send_f.at[layer, pl.ds(4 * i, 4)],
                dst_ref=recv_f.at[pl.ds(4 * (i ^ 1), 4)],
                send_sem=face_send.at[layer, i],
                recv_sem=face_recv.at[layer, i ^ 1],
                device_id=sides[i],
                device_id_type=MESH,
            )
            copy.start()
            copies.append(copy)
        for copy in copies:
            copy.wait()

        def halo(b, f):
            kind = kind_at[b, f]
            mine = faces[own_at[b, f]].astype(F32)
            far = recv_f[far_at[b, f]].astype(F32)
            zero = jnp.zeros((32, 128), F32)
            both = jnp.where(kind == 0, mine, jnp.where(kind > 0, far, zero))
            return [both[8 * t : 8 * t + 8] for t in range(4)]

        halos = [[halo(b, f) for f in range(6)] for b in range(4)]
        for b in range(4):
            for f in range(2):
                y_rows[f, b] = widen(halos[b][2 + f], none8, none8)
        for p in range(10):
            for pair in range(2):
                parts = [[], [], []]
                for b in (2 * pair, 2 * pair + 1):
                    if p == 0 or p == 9:
                        centre = widen(halos[b][0 if p == 0 else 1], none8, none8)
                        first = jnp.zeros((8, 640), F32)
                        last = first
                    else:
                        x = p - 1
                        tiles = [
                            nat[t, pl.ds(x * 32 + b * 8, 8), :] for t in range(4)
                        ]
                        z_low = halos[b][4][x % 4]
                        z_high = halos[b][5][x % 4]
                        if x >= 4:
                            z_low = half_turn(z_low)
                        else:
                            z_high = half_turn(z_high)
                        centre = widen(tiles, z_low, z_high)
                        first = jnp.broadcast_to(y_rows[0, b, pl.ds(x, 1), :], (8, 640))
                        last = jnp.broadcast_to(y_rows[1, b, pl.ds(x, 1), :], (8, 640))
                    parts[0].append(jnp.where(sub == 0, first, pltpu.roll(centre, 1, 0)))
                    parts[1].append(centre)
                    parts[2].append(jnp.where(sub == 7, last, pltpu.roll(centre, 7, 0)))
                for dy in range(3):
                    lhs[dy, pl.ds(p * 32 + pair * 16, 16), :] = jnp.concatenate(
                        parts[dy], axis=0
                    ).astype(BF16)

        gain = g_v[pl.ds(layer, 1), :]
        gain = jnp.concatenate([gain, gain], axis=1)
        for k in range(4):
            window = jnp.concatenate(
                [lhs[dy, :, pl.ds(128 * k, 256)] for dy in range(3)], axis=1
            )
            r = jnp.dot(window, banded[layer], preferred_element_type=F32)
            total = r[0:256, 0:128] + r[32:288, 128:256] + r[64:320, 256:384]
            square = total * total
            coarse = square.astype(BF16)
            fine = (square - coarse.astype(F32)).astype(BF16)
            mean = jnp.dot(
                jnp.concatenate([coarse, fine], axis=1), averager, preferred_element_type=F32
            )
            scaled = total * lax.rsqrt(mean + 1e-5) * gain
            keep = mask[:, pl.ds(128 * k, 128)] > 0.5
            done = jnp.where(keep, jnp.maximum(scaled, 0.0), 0.0)
            if layer == 0:
                nat[k] = done
            else:
                cells = done.reshape(8, 4, 8, 128)
                for b in range(4):
                    out[b, :, :, pl.ds(128 * k, 128)] = cells[:, b].astype(BF16)

    for copy in lists:
        copy.wait_send()
    cross_copy.wait_send()
    pair_copy.wait_send()


def local_program(groups, owners, features, block_loads, swap_counts, neighbours, occupancy, conv_weights, norm_gains):
    any_space = pl.BlockSpec(memory_space=pl.ANY)
    return pl.pallas_call(
        functools.partial(kernel, groups, owners),
        out_shape=jax.ShapeDtypeStruct((4, 8, 8, 512), BF16),
        in_specs=[any_space] * 7,
        out_specs=pl.BlockSpec(memory_space=pltpu.VMEM),
        scratch_shapes=[
            pltpu.VMEM((4, 64, 512), BF16),
            pltpu.VMEM((3, 64, 512), BF16),
            pltpu.VMEM((3, 64, 512), BF16),
            pltpu.SMEM((1,), I32),
            pltpu.SMEM((1, 2, owners), I32),
            pltpu.SMEM((4, 6), I32),
            pltpu.SMEM((4, 4, 6), I32),
            pltpu.SMEM((4, 6), I32),
            pltpu.SMEM((4, 6), I32),
            pltpu.SMEM((4, 6), I32),
            pltpu.VMEM((4, 512), I32),
            pltpu.VMEM((2, 27, 64, 64), BF16),
            pltpu.VMEM((2, 64), F32),
            pltpu.VMEM((2, 768, 384), BF16),
            pltpu.VMEM((256, 512), F32),
            pltpu.VMEM((4, 256, 128), F32),
            pltpu.VMEM((24, 32, 128), BF16),
            pltpu.VMEM((2, 16, 32, 128), BF16),
            pltpu.VMEM((16, 32, 128), BF16),
            pltpu.VMEM((16, 32, 128), BF16),
            pltpu.VMEM((3, 320, 640), BF16),
            pltpu.VMEM((2, 4, 8, 640), F32),
            pltpu.SemaphoreType.DMA((7,)),
            pltpu.SemaphoreType.DMA((4,)),
            pltpu.SemaphoreType.DMA((4,)),
            pltpu.SemaphoreType.DMA((2,)),
            pltpu.SemaphoreType.DMA((2,)),
            pltpu.SemaphoreType.DMA((2, 4)),
            pltpu.SemaphoreType.DMA((2, 4)),
        ],
        compiler_params=pltpu.CompilerParams(
            collective_id=0, has_side_effects=True, vmem_limit_bytes=40 * 1024 * 1024
        ),
    )(features.reshape(4, 64, 512), block_loads, swap_counts, neighbours, occupancy, conv_weights, norm_gains)


def solution(mesh):
    groups, owners = mesh.shape["grp"], mesh.shape["curve"]
    return jax.shard_map(
        functools.partial(local_program, groups, owners),
        mesh=mesh,
        in_specs=(
            P(("grp", "curve"), None, None, None),
            P(("grp", "curve")),
            P("grp", None, None),
            P(("grp", "curve"), None),
            P(("grp", "curve"), None),
            P(),
            P(),
        ),
        out_specs=P(("grp", "curve"), None, None, None),
        check_vma=False,
    )
```

time: 206 us -> 31.2 us (0.15)
  the two profiles are of different devices: /device:TPU:119 before, /device:TPU:2 now
where the time goes in v1:
time: 31.2 us; the launch traced here: 31 us
  Pallas kernels  25.4 us (81%)
  local copies, waits for them, and re-layouts  4.86 us (16%)
  between operations  0.69 us (2%)
    pallas_call x1, Pallas kernels, local_program(): pl.pallas_call(functools.partial(kernel, groups, owners), out_shape=jax.S...  25.4 us
    unnamed x13, local copies, waits for them, and re-layouts  4.86 us

profile of v1, /device:TPU:2, one launch (start us, length us, event | category | flops | bytes accessed | tf_op | source)
XLA Modules:
  0.0 31.0 jit_solution(9085458917584434606)
XLA Ops:
  0.0 0.0 copy-start.3
  0.7 0.0 copy-start.4
  0.7 0.0 copy-done.3
  0.7 0.7 %copy-done.4 = s32[1,2,32]{2,1,0:T(2,128)S(1)} copy-done((s32[1,2,32]{2,1,0:T(2,128)S(1)}, s32[1,2,32]{2,1,0:T(2,128)}, u32[]{:S(2)}) %copy-start.4) | copy-done | bytes 280
  1.3 0.0 copy-start
  1.4 1.2 %copy-done = bf16[2,27,64,64]{3,2,1,0:T(8,128)(2,1)S(1)} copy-done((bf16[2,27,64,64]{3,2,1,0:T(8,128)(2,1)S(1)}, bf16[2,27,64,64]{3,2,1,0:T(8,128)(2,1)}, u32[]{:S(2)}) %copy-start) | copy-done | bytes 442392
  2.5 0.0 copy-start.1
  2.5 0.9 %copy-done.1 = bf16[4,8,8,512]{3,2,1,0:T(8,128)(2,1)S(1)} copy-done((bf16[4,8,8,512]{3,2,1,0:T(8,128)(2,1)S(1)}, bf16[4,8,8,512]{3,2,1,0:T(8,128)(2,1)}, u32[]{:S(2)}) %copy-start.1) | copy-done | bytes 262168
  3.5 0.0 copy-start.2
  3.5 0.7 %copy-done.2 = s32[4,512]{1,0:T(4,128)S(1)} copy-done((s32[4,512]{1,0:T(4,128)S(1)}, s32[4,512]{1,0:T(4,128)}, u32[]{:S(2)}) %copy-start.2) | copy-done | bytes 8216
  4.2 0.0 copy-start.5
  4.2 0.7 %copy-done.5 = f32[2,64]{1,0:T(2,128)S(1)} copy-done((f32[2,64]{1,0:T(2,128)S(1)}, f32[2,64]{1,0:T(2,128)}, u32[]{:S(2)}) %copy-start.5) | copy-done | bytes 536
  4.8 25.4 %shard_map.73 = bf16[4,8,8,512]{3,2,1,0:T(8,128)(2,1)S(1)} custom-call(bf16[4,64,512]{2,1,0:T(8,128)(2,1)S(1)} %bitcast.1, s32[1]{0:T(128)S(6)} %copy.9.loads, s32[1,2,32]{2,1,0:T(2,128)S(1)} %copy-done.4, s32[4,6]{1,0:T(4,128)S(1)} %copy-done.3, s32[4,512]{1,0:T(4,128)S(1)} %copy-done.2, bf16[2,27,64,64]{3,2,1,0:T(8,128)(2,1)S(1)} %copy-done, ...), custom_call_target="tpu_custom_call" | custom-call | tf_op jit(solution)/shard_map/pallas_call | solution.py:368
  30.3 0.7 %copy.10 = bf16[4,8,8,512]{3,2,1,0:T(8,128)(2,1)} copy(bf16[4,8,8,512]{3,2,1,0:T(8,128)(2,1)S(1)} %shard_map.73) | data formatting | bytes 524288
Async XLA Ops:
  0.0 0.7 %copy-start.3 = (s32[4,6]{1,0:T(4,128)S(1)}, s32[4,6]{1,0:T(4,128)}, u32[]{:S(2)}) copy-start(s32[4,6]{1,0:T(4,128)} %nbrs.1) | copy-start | bytes 292
  0.7 0.7 %copy-start.4 = (s32[1,2,32]{2,1,0:T(2,128)S(1)}, s32[1,2,32]{2,1,0:T(2,128)}, u32[]{:S(2)}) copy-start(s32[1,2,32]{2,1,0:T(2,128)} %swaps.1) | copy-start | bytes 772
  1.3 1.2 %copy-start = (bf16[2,27,64,64]{3,2,1,0:T(8,128)(2,1)S(1)}, bf16[2,27,64,64]{3,2,1,0:T(8,128)(2,1)}, u32[]{:S(2)}) copy-start(bf16[2,27,64,64]{3,2,1,0:T(8,128)(2,1)} %wts.1) | copy-start | bytes 1327108
  2.5 0.9 %copy-start.1 = (bf16[4,8,8,512]{3,2,1,0:T(8,128)(2,1)S(1)}, bf16[4,8,8,512]{3,2,1,0:T(8,128)(2,1)}, u32[]{:S(2)}) copy-start(bf16[4,8,8,512]{3,2,1,0:T(8,128)(2,1)} %param.7) | copy-start | bytes 786436
  3.5 0.7 %copy-start.2 = (s32[4,512]{1,0:T(4,128)S(1)}, s32[4,512]{1,0:T(4,128)}, u32[]{:S(2)}) copy-start(s32[4,512]{1,0:T(4,128)} %occ.1) | copy-start | bytes 24580
  4.2 0.7 %copy-start.5 = (f32[2,64]{1,0:T(2,128)S(1)}, f32[2,64]{1,0:T(2,128)}, u32[]{:S(2)}) copy-start(f32[2,64]{1,0:T(2,128)} %gains.1) | copy-start | bytes 1540

commit v2 on v1

v2 whole, which is shorter than its diff:
```python
import functools
import types

import jax
import jax.numpy as jnp
from jax import lax
from jax.experimental import pallas as pl
from jax.experimental.pallas import tpu as pltpu
from jax.sharding import PartitionSpec as P

F32 = jnp.float32
BF16 = jnp.bfloat16
I32 = jnp.int32
MESH = pl.DeviceIdType.MESH

SCRATCH = dict(
    blocks=pltpu.VMEM((4, 64, 512), BF16),
    moved=pltpu.VMEM((3, 64, 512), BF16),
    outgoing=pltpu.VMEM((3, 64, 512), BF16),
    loads_s=pltpu.SMEM((1,), I32),
    swaps_s=pltpu.SMEM((1, 2, 32), I32),
    nbrs_s=pltpu.SMEM((4, 6), I32),
    asked_s=pltpu.SMEM((4, 4, 6), I32),
    own_at=pltpu.SMEM((4, 6), I32),
    far_at=pltpu.SMEM((4, 6), I32),
    kind_at=pltpu.SMEM((4, 6), I32),
    occ_v=pltpu.VMEM((4, 512), I32),
    w_v=pltpu.VMEM((2, 27, 64, 64), BF16),
    g_v=pltpu.VMEM((2, 64), F32),
    banded=pltpu.VMEM((2, 768, 384), BF16),
    mask=pltpu.VMEM((256, 512), F32),
    nat=pltpu.VMEM((4, 256, 128), F32),
    faces=pltpu.VMEM((24, 32, 128), BF16),
    send_f=pltpu.VMEM((2, 16, 32, 128), BF16),
    recv_first=pltpu.VMEM((16, 32, 128), BF16),
    recv_second=pltpu.VMEM((16, 32, 128), BF16),
    lhs=pltpu.VMEM((3, 320, 640), BF16),
    y_rows=pltpu.VMEM((2, 4, 8, 640), F32),
    in_sems=pltpu.SemaphoreType.DMA((7,)),
    list_send=pltpu.SemaphoreType.DMA((4,)),
    list_recv=pltpu.SemaphoreType.DMA((4,)),
    block_send=pltpu.SemaphoreType.DMA((2,)),
    block_recv=pltpu.SemaphoreType.DMA((2,)),
    face_send=pltpu.SemaphoreType.DMA((2, 4)),
    face_recv=pltpu.SemaphoreType.DMA((2, 4)),
)
OPERANDS = ("feat", "loads", "swaps", "nbrs", "occ", "wts", "gains", "out")


def lanes_low():
    return lax.broadcasted_iota(I32, (8, 128), 1) < 64


def half_turn(tile):
    return pltpu.roll(tile, 64, 1)


def widen(tiles, low_side, high_side):
    low = lanes_low()
    turned = [half_turn(t) for t in tiles]
    out = [jnp.where(low, low_side, turned[0])]
    for t in range(1, 4):
        out.append(jnp.where(low, turned[t - 1], turned[t]))
    out.append(jnp.where(low, turned[3], high_side))
    return jnp.concatenate(out, axis=1)


def build_weights(r):
    zero_w = jnp.zeros((64, 64), BF16)
    for layer in range(2):
        for dx in range(3):
            for dy in range(3):
                w = [r.w_v[layer, dx * 9 + dy * 3 + dz] for dz in range(3)]
                rows = [(w[0], zero_w), (w[1], w[0]), (w[2], w[1]), (zero_w, w[2])]
                for zi in range(4):
                    r.banded[layer, pl.ds((dy * 4 + zi) * 64, 64), pl.ds(dx * 128, 128)] = (
                        jnp.concatenate(rows[zi], axis=1)
                    )


def settle_places(r, owners, own, odd, load, tail):
    swap = r.swaps_s[0, 0, own - lax.rem(own, 2)]
    flow_in = jnp.where(own > 0, r.swaps_s[0, 1, jnp.maximum(own - 1, 0)], 0)
    flow_out = jnp.where(own < owners - 1, r.swaps_s[0, 1, own], 0)
    first_load = load + jnp.where(odd, swap, -swap)
    came = jnp.maximum(flow_in, 0)
    dropped = jnp.maximum(-flow_in, 0)
    middle = first_load - dropped - jnp.maximum(flow_out, 0)
    taken = jnp.maximum(-flow_out, 0)
    final = first_load + flow_in - flow_out
    came_at = jnp.where(odd, jnp.where(swap > 0, 4, jnp.where(swap < 0, 0, 5)), 6)
    taken_at = jnp.where(odd, 6, jnp.where(swap > 0, tail, jnp.where(swap < 0, 5, 4)))
    places = []
    for j in range(4):
        i = j - came + dropped
        even_at = jnp.where(i < load - jnp.maximum(swap, 0), i, 4)
        odd_at = jnp.where((swap > 0) & (i == 0), 5, i - swap)
        kept_at = jnp.where(odd, odd_at, even_at)
        at = jnp.where(
            j < came,
            came_at,
            jnp.where(j < came + middle, kept_at, jnp.where(j < came + middle + taken, taken_at, 0)),
        )
        places.append(jnp.clip(at, 0, 6))
    return places, final


def build_mask(r, final):
    block_no = lax.broadcasted_iota(I32, (4, 512), 0)
    occupied = jnp.where((block_no < final) & (r.occ_v[...] > 0), 1.0, 0.0).astype(F32)
    lane3 = lax.broadcasted_iota(I32, (4, 8, 128), 2)
    sub3 = lax.broadcasted_iota(I32, (4, 8, 128), 1)
    strips = []
    for x in range(8):
        strip = occupied[:, 128 * (x // 2) : 128 * (x // 2) + 128]
        wide = jnp.broadcast_to(strip[:, None, :], (4, 8, 128))
        pick = (lane3 // 8) == (sub3 + 8 * (x % 2))
        strips.append(jnp.where(pick, wide, 0.0).reshape(32, 128))
    strips = jnp.concatenate(strips, axis=0).astype(BF16)
    spread = jnp.where(
        lax.rem(lax.broadcasted_iota(I32, (128, 512), 0), 8)
        == lax.broadcasted_iota(I32, (128, 512), 1) // 64,
        1.0,
        0.0,
    ).astype(BF16)
    r.mask[...] = jnp.dot(strips, spread, preferred_element_type=F32)


def rank_halos(r):
    def rank_step(b, counts):
        counts = list(counts)
        for f in range(6):
            v = r.nbrs_s[b, f]
            s = lax.shift_right_arithmetic(v, 2)
            rank = jnp.int32(0)
            for i in range(4):
                hit = s == i + 1
                rank = jnp.where(hit, 4 * i + counts[i], rank)
                counts[i] = counts[i] + hit.astype(I32)
            r.kind_at[b, f] = s
            r.own_at[b, f] = jnp.where(v >= 0, (v & 3) * 6 + (f ^ 1), 0)
            r.far_at[b, f] = jnp.clip(rank, 0, 15)
        return tuple(counts)

    lax.fori_loop(0, 4, rank_step, (jnp.int32(0),) * 4)


def rank_asked(r):
    def ask_step(b, state):
        state = [list(row) for row in state]
        for f in range(6):
            for i in range(4):
                v = r.asked_s[i, b, f]
                count = state[i][4]
                hit = lax.shift_right_arithmetic(v, 2) == (i ^ 1) + 1
                face = (v & 3) * 6 + (f ^ 1)
                for j in range(4):
                    state[i][j] = jnp.where(hit & (count == j), face, state[i][j])
                state[i][4] = count + hit.astype(I32)
        return tuple(tuple(row) for row in state)

    return lax.fori_loop(0, 4, ask_step, ((jnp.int32(0),) * 5,) * 4)


def settle(r, places):
    for j in range(4):
        mine = r.blocks[jnp.minimum(places[j], 3)].astype(F32)
        other = r.moved[jnp.maximum(places[j] - 4, 0)].astype(F32)
        block = jnp.where(places[j] < 4, mine, other)
        for x in range(8):
            rows = pl.ds(x * 32 + j * 8, 8)
            kept = jnp.where(r.mask[rows, :] > 0.5, block[8 * x : 8 * x + 8], 0.0)
            for t in range(4):
                r.nat[t, rows, :] = kept[:, 128 * t : 128 * t + 128]


def build_faces(r):
    low = lanes_low()
    for b in range(4):
        for f in range(2):
            face = [r.nat[t, pl.ds(7 * f * 32 + b * 8, 8), :] for t in range(4)]
            r.faces[b * 6 + f] = jnp.concatenate(face, axis=0).astype(BF16)
            face = [r.nat[t, pl.ds(b * 8 + 7 * f, 8, stride=32), :] for t in range(4)]
            r.faces[b * 6 + 2 + f] = jnp.concatenate(face, axis=0).astype(BF16)
        for f in range(2):
            face = []
            for x in range(4):
                here = r.nat[3 * f, pl.ds(x * 32 + b * 8, 8), :]
                there = r.nat[3 * f, pl.ds((x + 4) * 32 + b * 8, 8), :]
                if f == 0:
                    there = half_turn(there)
                else:
                    here = half_turn(here)
                face.append(jnp.where(low, here, there))
            r.faces[b * 6 + 4 + f] = jnp.concatenate(face, axis=0).astype(BF16)


def pick_faces(r, layer, asked):
    for i in range(4):
        for j in range(4):
            r.send_f[layer, 4 * i + j] = r.faces[asked[i][j]]


def read_halos(r, recv_f):
    def halo(b, f):
        kind = r.kind_at[b, f]
        mine = r.faces[r.own_at[b, f]].astype(F32)
        far = recv_f[r.far_at[b, f]].astype(F32)
        zero = jnp.zeros((32, 128), F32)
        both = jnp.where(kind == 0, mine, jnp.where(kind > 0, far, zero))
        return [both[8 * t : 8 * t + 8] for t in range(4)]

    return [[halo(b, f) for f in range(6)] for b in range(4)]


def build_lhs(r, halos):
    sub = lax.broadcasted_iota(I32, (8, 640), 0)
    none8 = jnp.zeros((8, 128), F32)
    for b in range(4):
        for f in range(2):
            r.y_rows[f, b] = widen(halos[b][2 + f], none8, none8)
    for p in range(10):
        for pair in range(2):
            parts = [[], [], []]
            for b in (2 * pair, 2 * pair + 1):
                if p == 0 or p == 9:
                    centre = widen(halos[b][0 if p == 0 else 1], none8, none8)
                    first = jnp.zeros((8, 640), F32)
                    last = first
                else:
                    x = p - 1
                    tiles = [r.nat[t, pl.ds(x * 32 + b * 8, 8), :] for t in range(4)]
                    z_low = halos[b][4][x % 4]
                    z_high = halos[b][5][x % 4]
                    if x >= 4:
                        z_low = half_turn(z_low)
                    else:
                        z_high = half_turn(z_high)
                    centre = widen(tiles, z_low, z_high)
                    first = jnp.broadcast_to(r.y_rows[0, b, pl.ds(x, 1), :], (8, 640))
                    last = jnp.broadcast_to(r.y_rows[1, b, pl.ds(x, 1), :], (8, 640))
                parts[0].append(jnp.where(sub == 0, first, pltpu.roll(centre, 1, 0)))
                parts[1].append(centre)
                parts[2].append(jnp.where(sub == 7, last, pltpu.roll(centre, 7, 0)))
            for dy in range(3):
                r.lhs[dy, pl.ds(p * 32 + pair * 16, 16), :] = jnp.concatenate(
                    parts[dy], axis=0
                ).astype(BF16)


def convolve(r, layer):
    group_lane = lax.broadcasted_iota(I32, (256, 128), 1) // 64
    group_row = lax.rem(lax.broadcasted_iota(I32, (256, 128), 0), 128) // 64
    averager = jnp.where(group_lane == group_row, 1.0 / 64.0, 0.0).astype(BF16)
    gain = r.g_v[pl.ds(layer, 1), :]
    gain = jnp.concatenate([gain, gain], axis=1)
    for k in range(4):
        window = jnp.concatenate([r.lhs[dy, :, pl.ds(128 * k, 256)] for dy in range(3)], axis=1)
        three = jnp.dot(window, r.banded[layer], preferred_element_type=F32)
        total = three[0:256, 0:128] + three[32:288, 128:256] + three[64:320, 256:384]
        square = total * total
        coarse = square.astype(BF16)
        fine = (square - coarse.astype(F32)).astype(BF16)
        mean = jnp.dot(
            jnp.concatenate([coarse, fine], axis=1), averager, preferred_element_type=F32
        )
        scaled = total * lax.rsqrt(mean + 1e-5) * gain
        keep = r.mask[:, pl.ds(128 * k, 128)] > 0.5
        done = jnp.where(keep, jnp.maximum(scaled, 0.0), 0.0)
        if layer == 0:
            r.nat[k] = done
        else:
            cells = done.reshape(8, 4, 8, 128)
            for b in range(4):
                r.out[b, :, :, pl.ds(128 * k, 128)] = cells[:, b].astype(BF16)


def kernel(groups, owners, *refs):
    r = types.SimpleNamespace(**dict(zip(OPERANDS + tuple(SCRATCH), refs)))
    grp = lax.axis_index("grp")
    own = lax.axis_index("curve")
    odd = lax.rem(own, 2) == 1
    sides = (
        (grp, jnp.maximum(own - 1, 0)),
        (grp, jnp.minimum(own + 1, owners - 1)),
        (jnp.maximum(grp - 1, 0), own),
        (jnp.minimum(grp + 1, groups - 1), own),
    )
    there = (own > 0, own < owners - 1, grp > 0, grp < groups - 1)

    def for_sides(step):
        for i in range(4):
            pl.when(there[i])(functools.partial(step, i))

    local = [
        pltpu.make_async_copy(source, target, r.in_sems.at[i])
        for i, (source, target) in enumerate(
            (
                (r.feat, r.blocks),
                (r.loads, r.loads_s),
                (r.swaps, r.swaps_s),
                (r.nbrs, r.nbrs_s),
                (r.occ, r.occ_v),
                (r.wts, r.w_v),
                (r.gains, r.g_v),
            )
        )
    ]
    for copy in local:
        copy.start()

    barrier = pltpu.get_barrier_semaphore()
    for_sides(
        lambda i: pl.semaphore_signal(barrier, inc=1, device_id=sides[i], device_id_type=MESH)
    )
    pl.semaphore_wait(barrier, sum(flag.astype(I32) for flag in there))

    lists = [
        pltpu.make_async_remote_copy(
            src_ref=r.nbrs,
            dst_ref=r.asked_s.at[i ^ 1],
            send_sem=r.list_send.at[i],
            recv_sem=r.list_recv.at[i ^ 1],
            device_id=sides[i],
            device_id_type=MESH,
        )
        for i in range(4)
    ]
    for_sides(lambda i: lists[i].start())

    local[1].wait()
    local[0].wait()
    load = r.loads_s[0]
    tail = jnp.maximum(load - 1, 0)
    r.outgoing[2] = r.blocks[jnp.where(odd, tail, 0)]
    partner = (grp, own + 1 - 2 * lax.rem(own, 2))
    across = (grp, jnp.clip(own - 1 + 2 * lax.rem(own, 2), 0, owners - 1))
    has_across = (own > 0) & (own < owners - 1)
    cross_copy = pltpu.make_async_remote_copy(
        src_ref=r.outgoing.at[pl.ds(2, 1)],
        dst_ref=r.moved.at[pl.ds(2, 1)],
        send_sem=r.block_send.at[0],
        recv_sem=r.block_recv.at[0],
        device_id=across,
        device_id_type=MESH,
    )
    pl.when(has_across)(cross_copy.start)
    r.outgoing[0] = r.blocks[jnp.where(odd, 0, jnp.maximum(load - 2, 0))]
    r.outgoing[1] = r.blocks[jnp.where(odd, 1, tail)]
    pair_copy = pltpu.make_async_remote_copy(
        src_ref=r.outgoing.at[pl.ds(0, 2)],
        dst_ref=r.moved.at[pl.ds(0, 2)],
        send_sem=r.block_send.at[1],
        recv_sem=r.block_recv.at[1],
        device_id=partner,
        device_id_type=MESH,
    )
    pair_copy.start()

    for copy in local[2:]:
        copy.wait()
    build_weights(r)
    places, final = settle_places(r, owners, own, odd, load, tail)
    build_mask(r, final)
    rank_halos(r)
    for i in range(4):

        @pl.when(jnp.logical_not(there[i]))
        def _():
            for b in range(4):
                for f in range(6):
                    r.asked_s[i, b, f] = -1

    for_sides(lambda i: lists[i ^ 1].wait_recv())
    asked = rank_asked(r)

    pl.when(has_across)(cross_copy.wait_recv)
    pair_copy.wait_recv()
    settle(r, places)

    for layer in range(2):
        recv_f = (r.recv_first, r.recv_second)[layer]
        build_faces(r)
        pick_faces(r, layer, asked)
        copies = [
            pltpu.make_async_remote_copy(
                src_ref=r.send_f.at[layer, pl.ds(4 * i, 4)],
                dst_ref=recv_f.at[pl.ds(4 * (i ^ 1), 4)],
                send_sem=r.face_send.at[layer, i],
                recv_sem=r.face_recv.at[layer, i ^ 1],
                device_id=sides[i],
                device_id_type=MESH,
            )
            for i in range(4)
        ]
        for_sides(lambda i: copies[i].start())
        for_sides(lambda i: copies[i].wait_send())
        for_sides(lambda i: copies[i ^ 1].wait_recv())

        build_lhs(r, read_halos(r, recv_f))
        convolve(r, layer)

    for_sides(lambda i: lists[i].wait_send())
    pl.when(has_across)(cross_copy.wait_send)
    pair_copy.wait_send()


def local_program(groups, owners, features, block_loads, swap_counts, neighbours, occupancy, conv_weights, norm_gains):
    any_space = pl.BlockSpec(memory_space=pl.ANY)
    return pl.pallas_call(
        functools.partial(kernel, groups, owners),
        out_shape=jax.ShapeDtypeStruct((4, 8, 8, 512), BF16),
        in_specs=[any_space] * 7,
        out_specs=pl.BlockSpec(memory_space=pltpu.VMEM),
        scratch_shapes=list(SCRATCH.values()),
        compiler_params=pltpu.CompilerParams(
            collective_id=0, has_side_effects=True, vmem_limit_bytes=60 * 1024 * 1024
        ),
    )(
        features.reshape(4, 64, 512),
        block_loads,
        swap_counts,
        neighbours,
        occupancy,
        conv_weights,
        norm_gains,
    )


def solution(mesh):
    groups, owners = mesh.shape["grp"], mesh.shape["curve"]
    return jax.shard_map(
        functools.partial(local_program, groups, owners),
        mesh=mesh,
        in_specs=(
            P(("grp", "curve"), None, None, None),
            P(("grp", "curve")),
            P("grp", None, None),
            P(("grp", "curve"), None),
            P(("grp", "curve"), None),
            P(),
            P(),
        ),
        out_specs=P(("grp", "curve"), None, None, None),
        check_vma=False,
    )
```

time: 31.2 us -> 25.3 us (0.81)
  the two profiles are of different devices: /device:TPU:2 before, /device:TPU:119 now
where the time goes in v2:
time: 25.3 us; the launch traced here: 25.2 us
  Pallas kernels  22.9 us (91%)
  local copies, waits for them, and re-layouts  1.67 us (7%)
  between operations  0.66 us (3%)
    pallas_call x1, Pallas kernels, local_program(): pl.pallas_call(functools.partial(kernel, groups, owners), out_shape=jax.S...  22.9 us
    unnamed x1, local copies, waits for them, and re-layouts  1.67 us

profile of v2, /device:TPU:119, one launch (start us, length us, event | category | flops | bytes accessed | tf_op | source)
XLA Modules:
  0.0 25.2 jit_solution(14618601772043784697)
XLA Ops:
  0.7 22.9 %shard_map.73 = bf16[4,8,8,512]{3,2,1,0:T(8,128)(2,1)} custom-call(bf16[4,64,512]{2,1,0:T(8,128)(2,1)} %bitcast.1, s32[1]{0:T(128)S(6)} %copy.9.refs_1_, s32[1,2,32]{2,1,0:T(2,128)} %refs_2_.1, s32[4,6]{1,0:T(4,128)} %refs_3_.1, s32[4,512]{1,0:T(4,128)} %refs_4_.1, bf16[2,27,64,64]{3,2,1,0:T(8,128)(2,1)} %refs_5_.1, f32[2,64]{1,0:T(2,128)} %refs_6_.1), custom_call_target="tpu_custom_call" | custom-call | tf_op jit(solution)/shard_map/pallas_call | solution.py:410
  23.5 1.7 %copy.10 = bf16[4,8,8,512]{3,2,1,0:T(8,128)(2,1)} copy(bf16[4,8,8,512]{3,2,1,0:T(8,128)(2,1)} %shard_map.73) | data formatting | bytes 524288

commit v3 on v2

--- a/solution.py
+++ b/solution.py
@@ -34,8 +34,12 @@
     send_f=pltpu.VMEM((2, 16, 32, 128), BF16),
     recv_first=pltpu.VMEM((16, 32, 128), BF16),
     recv_second=pltpu.VMEM((16, 32, 128), BF16),
-    lhs=pltpu.VMEM((3, 320, 640), BF16),
-    y_rows=pltpu.VMEM((2, 4, 8, 640), F32),
+    lhs=pltpu.VMEM((3, 256, 640), BF16),
+    x_lhs=pltpu.VMEM((2, 3, 32, 640), BF16),
+    y_lhs=pltpu.VMEM((2, 32, 640), BF16),
+    z_lhs=pltpu.VMEM((3, 256, 128), BF16),
+    acc=pltpu.VMEM((4, 256, 128), F32),
+    y_add=pltpu.VMEM((2, 4, 4, 8, 128), F32),
     in_sems=pltpu.SemaphoreType.DMA((7,)),
     list_send=pltpu.SemaphoreType.DMA((4,)),
     list_recv=pltpu.SemaphoreType.DMA((4,)),
@@ -213,51 +217,129 @@
     return [[halo(b, f) for f in range(6)] for b in range(4)]
 
 
-def build_lhs(r, halos):
-    sub = lax.broadcasted_iota(I32, (8, 640), 0)
+def shifted_rows(tile):
+    sub = lax.broadcasted_iota(I32, tile.shape, 0)
+    return (
+        jnp.where(sub == 0, 0.0, pltpu.roll(tile, 1, 0)),
+        tile,
+        jnp.where(sub == 7, 0.0, pltpu.roll(tile, 7, 0)),
+    )
+
+
+def put_pair(ref, at, row, tiles):
+    ref[at + (pl.ds(row, 16), slice(None))] = jnp.concatenate(tiles, axis=0).astype(BF16)
+
+
+def build_lhs(r):
     none8 = jnp.zeros((8, 128), F32)
-    for b in range(4):
-        for f in range(2):
-            r.y_rows[f, b] = widen(halos[b][2 + f], none8, none8)
-    for p in range(10):
+    for x in range(8):
         for pair in range(2):
-            parts = [[], [], []]
+            row = x * 32 + pair * 16
+            parts = []
             for b in (2 * pair, 2 * pair + 1):
-                if p == 0 or p == 9:
-                    centre = widen(halos[b][0 if p == 0 else 1], none8, none8)
-                    first = jnp.zeros((8, 640), F32)
-                    last = first
-                else:
-                    x = p - 1
-                    tiles = [r.nat[t, pl.ds(x * 32 + b * 8, 8), :] for t in range(4)]
-                    z_low = halos[b][4][x % 4]
-                    z_high = halos[b][5][x % 4]
-                    if x >= 4:
-                        z_low = half_turn(z_low)
-                    else:
-                        z_high = half_turn(z_high)
-                    centre = widen(tiles, z_low, z_high)
-                    first = jnp.broadcast_to(r.y_rows[0, b, pl.ds(x, 1), :], (8, 640))
-                    last = jnp.broadcast_to(r.y_rows[1, b, pl.ds(x, 1), :], (8, 640))
-                parts[0].append(jnp.where(sub == 0, first, pltpu.roll(centre, 1, 0)))
-                parts[1].append(centre)
-                parts[2].append(jnp.where(sub == 7, last, pltpu.roll(centre, 7, 0)))
+                tiles = [r.nat[t, pl.ds(x * 32 + b * 8, 8), :] for t in range(4)]
+                parts.append(shifted_rows(widen(tiles, none8, none8)))
             for dy in range(3):
-                r.lhs[dy, pl.ds(p * 32 + pair * 16, 16), :] = jnp.concatenate(
-                    parts[dy], axis=0
-                ).astype(BF16)
-
-
-def convolve(r, layer):
+                put_pair(r.lhs, (dy,), row, [part[dy] for part in parts])
+
+
+def over_dx(three):
+    rim = jnp.zeros((32, 128), F32)
+    return (
+        three[:, 128:256]
+        + jnp.concatenate([rim, three[0:224, 0:128]], axis=0)
+        + jnp.concatenate([three[32:256, 256:384], rim], axis=0)
+    )
+
+
+def convolve_own(r, layer):
+    for k in range(4):
+        window = jnp.concatenate([r.lhs[dy, :, pl.ds(128 * k, 256)] for dy in range(3)], axis=1)
+        three = jnp.dot(window, r.banded[layer], preferred_element_type=F32)
+        r.acc[k] = over_dx(three)
+
+
+def add_halos(r, layer, halos):
+    none8 = jnp.zeros((8, 128), F32)
+    low = lanes_low()
+    for f in range(2):
+        for pair in range(2):
+            wide = [widen(halos[b][f], none8, none8) for b in (2 * pair, 2 * pair + 1)]
+            parts = [shifted_rows(tile) for tile in wide]
+            for dy in range(3):
+                put_pair(r.x_lhs, (f, dy), 16 * pair, [part[dy] for part in parts])
+            wide = [widen(halos[b][2 + f], none8, none8) for b in (2 * pair, 2 * pair + 1)]
+            put_pair(r.y_lhs, (f,), 16 * pair, wide)
+    for pair in range(2):
+        parts = [[None] * 2 for _ in range(8)]
+        for i, b in enumerate((2 * pair, 2 * pair + 1)):
+            for x in range(4):
+                first, last = halos[b][4][x], halos[b][5][x]
+                parts[x][i] = shifted_rows(jnp.where(low, first, half_turn(last)))
+                parts[x + 4][i] = shifted_rows(jnp.where(low, half_turn(first), last))
+        for x in range(8):
+            for dy in range(3):
+                put_pair(r.z_lhs, (dy,), x * 32 + 16 * pair, [part[dy] for part in parts[x]])
+
+    for f in range(2):
+        window = jnp.concatenate(
+            [
+                jnp.concatenate([r.x_lhs[f, dy, :, pl.ds(128 * k, 256)] for dy in range(3)], axis=1)
+                for k in range(4)
+            ],
+            axis=0,
+        )
+        part = jnp.dot(
+            window, r.banded[layer, :, pl.ds(256 * f, 128)], preferred_element_type=F32
+        )
+        for k in range(4):
+            rows = pl.ds(224 * f, 32)
+            r.acc[k, rows, :] = r.acc[k, rows, :] + part[32 * k : 32 * k + 32]
+
+        window = jnp.concatenate([r.y_lhs[f, :, pl.ds(128 * k, 256)] for k in range(4)], axis=0)
+        part = jnp.dot(
+            window, r.banded[layer, pl.ds(512 * f, 256), :], preferred_element_type=F32
+        )
+        for k in range(4):
+            for b in range(4):
+                tile = part[32 * k + 8 * b : 32 * k + 8 * b + 8]
+                r.y_add[f, k, b] = (
+                    shifted_rows(tile[:, 0:128])[0]
+                    + tile[:, 128:256]
+                    + shifted_rows(tile[:, 256:384])[2]
+                )
+
+    window = jnp.concatenate([r.z_lhs[dy] for dy in range(3)], axis=1)
+    ends = jnp.concatenate(
+        [r.banded[layer, pl.ds(dy * 256 + at, 64), :] for dy in range(3) for at in (0, 192)], axis=0
+    )
+    z_add = over_dx(jnp.dot(window, ends, preferred_element_type=F32))
+
+    sub = lax.broadcasted_iota(I32, (8, 128), 0)
+    for k in range(4):
+        for x in range(8):
+            for b in range(4):
+                rows = pl.ds(x * 32 + b * 8, 8)
+                first = jnp.broadcast_to(r.y_add[0, k, b, pl.ds(x, 1), :], (8, 128))
+                last = jnp.broadcast_to(r.y_add[1, k, b, pl.ds(x, 1), :], (8, 128))
+                tile = r.acc[k, rows, :]
+                tile = tile + jnp.where(sub == 0, first, jnp.where(sub == 7, last, 0.0))
+                side = z_add[x * 32 + b * 8 : x * 32 + b * 8 + 8]
+                if k == 0:
+                    tile = tile + jnp.where(low, side, 0.0)
+                if k == 3:
+                    tile = tile + jnp.where(low, 0.0, side)
+                r.acc[k, rows, :] = tile
+
+
+def finish(r, layer):
     group_lane = lax.broadcasted_iota(I32, (256, 128), 1) // 64
     group_row = lax.rem(lax.broadcasted_iota(I32, (256, 128), 0), 128) // 64
     averager = jnp.where(group_lane == group_row, 1.0 / 64.0, 0.0).astype(BF16)
     gain = r.g_v[pl.ds(layer, 1), :]
     gain = jnp.concatenate([gain, gain], axis=1)
     for k in range(4):
-        window = jnp.concatenate([r.lhs[dy, :, pl.ds(128 * k, 256)] for dy in range(3)], axis=1)
-        three = jnp.dot(window, r.banded[layer], preferred_element_type=F32)
-        total = three[0:256, 0:128] + three[32:288, 128:256] + three[64:320, 256:384]
+        total = r.acc[k]
         square = total * total
         coarse = square.astype(BF16)
         fine = (square - coarse.astype(F32)).astype(BF16)
@@ -378,6 +460,7 @@
     pair_copy.wait_recv()
     settle(r, places)
 
+    sent = []
     for layer in range(2):
         recv_f = (r.recv_first, r.recv_second)[layer]
         build_faces(r)
@@ -394,27 +477,31 @@
             for i in range(4)
         ]
         for_sides(lambda i: copies[i].start())
-        for_sides(lambda i: copies[i].wait_send())
+
+        build_lhs(r)
+        convolve_own(r, layer)
         for_sides(lambda i: copies[i ^ 1].wait_recv())
-
-        build_lhs(r, read_halos(r, recv_f))
-        convolve(r, layer)
+        add_halos(r, layer, read_halos(r, recv_f))
+        finish(r, layer)
+        sent += copies
 
     for_sides(lambda i: lists[i].wait_send())
+    for_sides(lambda i: sent[i].wait_send())
+    for_sides(lambda i: sent[4 + i].wait_send())
     pl.when(has_across)(cross_copy.wait_send)
     pair_copy.wait_send()
 
 
 def local_program(groups, owners, features, block_loads, swap_counts, neighbours, occupancy, conv_weights, norm_gains):
-    any_space = pl.BlockSpec(memory_space=pl.ANY)
+    in_hbm = pl.BlockSpec(memory_space=pltpu.HBM)
     return pl.pallas_call(
         functools.partial(kernel, groups, owners),
         out_shape=jax.ShapeDtypeStruct((4, 8, 8, 512), BF16),
-        in_specs=[any_space] * 7,
+        in_specs=[in_hbm] * 7,
         out_specs=pl.BlockSpec(memory_space=pltpu.VMEM),
         scratch_shapes=list(SCRATCH.values()),
         compiler_params=pltpu.CompilerParams(
-            collective_id=0, has_side_effects=True, vmem_limit_bytes=60 * 1024 * 1024
+            collective_id=0, has_side_effects=True, vmem_limit_bytes=32 * 1024 * 1024
         ),
     )(
         features.reshape(4, 64, 512),

time: 25.3 us -> 25.5 us (level)
  Pallas kernels: 22.9 us -> 19.6 us
  local copies, waits for them, and re-layouts: 1.67 us -> 4.86 us
    pallas_call x1, Pallas kernels: 22.9 us -> 19.6 us  [local_program(): pl.pallas_call(functools.partial(kernel, groups, owners), out_shape=jax.S...]
    unnamed x1 -> x13, local copies, waits for them, and re-layouts: 1.67 us -> 4.86 us
where the time goes in v3:
time: 25.5 us; the launch traced here: 25.2 us
  Pallas kernels  19.6 us (77%)
  local copies, waits for them, and re-layouts  4.86 us (19%)
  between operations  0.69 us (3%)
    pallas_call x1, Pallas kernels, local_program(): pl.pallas_call(functools.partial(kernel, groups, owners), out_shape=jax.S...  19.6 us
    unnamed x13, local copies, waits for them, and re-layouts  4.86 us

profile of v3, /device:TPU:119, one launch (start us, length us, event | category | flops | bytes accessed | tf_op | source)
XLA Modules:
  0.0 25.2 jit_solution(8390959935954386626)
XLA Ops:
  0.0 0.0 copy-start.3
  0.7 0.0 copy-start.4
  0.7 0.0 copy-done.3
  0.7 0.7 %copy-done.4 = s32[1,2,32]{2,1,0:T(2,128)S(1)} copy-done((s32[1,2,32]{2,1,0:T(2,128)S(1)}, s32[1,2,32]{2,1,0:T(2,128)}, u32[]{:S(2)}) %copy-start.4) | copy-done | bytes 280
  1.3 0.0 copy-start
  1.4 1.2 %copy-done = bf16[2,27,64,64]{3,2,1,0:T(8,128)(2,1)S(1)} copy-done((bf16[2,27,64,64]{3,2,1,0:T(8,128)(2,1)S(1)}, bf16[2,27,64,64]{3,2,1,0:T(8,128)(2,1)}, u32[]{:S(2)}) %copy-start) | copy-done | bytes 442392
  2.5 0.0 copy-start.1
  2.5 0.9 %copy-done.1 = bf16[4,8,8,512]{3,2,1,0:T(8,128)(2,1)S(1)} copy-done((bf16[4,8,8,512]{3,2,1,0:T(8,128)(2,1)S(1)}, bf16[4,8,8,512]{3,2,1,0:T(8,128)(2,1)}, u32[]{:S(2)}) %copy-start.1) | copy-done | bytes 262168
  3.5 0.0 copy-start.2
  3.5 0.7 %copy-done.2 = s32[4,512]{1,0:T(4,128)S(1)} copy-done((s32[4,512]{1,0:T(4,128)S(1)}, s32[4,512]{1,0:T(4,128)}, u32[]{:S(2)}) %copy-start.2) | copy-done | bytes 8216
  4.2 0.0 copy-start.5
  4.2 0.7 %copy-done.5 = f32[2,64]{1,0:T(2,128)S(1)} copy-done((f32[2,64]{1,0:T(2,128)S(1)}, f32[2,64]{1,0:T(2,128)}, u32[]{:S(2)}) %copy-start.5) | copy-done | bytes 536
  4.8 19.6 %shard_map.73 = bf16[4,8,8,512]{3,2,1,0:T(8,128)(2,1)S(1)} custom-call(bf16[4,64,512]{2,1,0:T(8,128)(2,1)S(1)} %bitcast.1, s32[1]{0:T(128)S(6)} %copy.9.refs_1_, s32[1,2,32]{2,1,0:T(2,128)S(1)} %copy-done.4, s32[4,6]{1,0:T(4,128)S(1)} %copy-done.3, s32[4,512]{1,0:T(4,128)S(1)} %copy-done.2, bf16[2,27,64,64]{3,2,1,0:T(8,128)(2,1)S(1)} %copy-done, ...), custom_call_target="tpu_custom_call" | custom-call | tf_op jit(solution)/shard_map/pallas_call | solution.py:497
  24.5 0.7 %copy.10 = bf16[4,8,8,512]{3,2,1,0:T(8,128)(2,1)} copy(bf16[4,8,8,512]{3,2,1,0:T(8,128)(2,1)S(1)} %shard_map.73) | data formatting | bytes 524288
Async XLA Ops:
  0.0 0.7 %copy-start.3 = (s32[4,6]{1,0:T(4,128)S(1)}, s32[4,6]{1,0:T(4,128)}, u32[]{:S(2)}) copy-start(s32[4,6]{1,0:T(4,128)} %refs_3_.1) | copy-start | bytes 292
  0.7 0.7 %copy-start.4 = (s32[1,2,32]{2,1,0:T(2,128)S(1)}, s32[1,2,32]{2,1,0:T(2,128)}, u32[]{:S(2)}) copy-start(s32[1,2,32]{2,1,0:T(2,128)} %refs_2_.1) | copy-start | bytes 772
  1.3 1.2 %copy-start = (bf16[2,27,64,64]{3,2,1,0:T(8,128)(2,1)S(1)}, bf16[2,27,64,64]{3,2,1,0:T(8,128)(2,1)}, u32[]{:S(2)}) copy-start(bf16[2,27,64,64]{3,2,1,0:T(8,128)(2,1)} %refs_5_.1) | copy-start | bytes 1327108
  2.5 0.9 %copy-start.1 = (bf16[4,8,8,512]{3,2,1,0:T(8,128)(2,1)S(1)}, bf16[4,8,8,512]{3,2,1,0:T(8,128)(2,1)}, u32[]{:S(2)}) copy-start(bf16[4,8,8,512]{3,2,1,0:T(8,128)(2,1)} %param.7) | copy-start | bytes 786436
  3.5 0.7 %copy-start.2 = (s32[4,512]{1,0:T(4,128)S(1)}, s32[4,512]{1,0:T(4,128)}, u32[]{:S(2)}) copy-start(s32[4,512]{1,0:T(4,128)} %refs_4_.1) | copy-start | bytes 24580
  4.2 0.7 %copy-start.5 = (f32[2,64]{1,0:T(2,128)S(1)}, f32[2,64]{1,0:T(2,128)}, u32[]{:S(2)}) copy-start(f32[2,64]{1,0:T(2,128)} %refs_6_.1) | copy-start | bytes 1540

commit v4 on v3

--- a/solution.py
+++ b/solution.py
@@ -17,7 +17,6 @@
     blocks=pltpu.VMEM((4, 64, 512), BF16),
     moved=pltpu.VMEM((3, 64, 512), BF16),
     outgoing=pltpu.VMEM((3, 64, 512), BF16),
-    loads_s=pltpu.SMEM((1,), I32),
     swaps_s=pltpu.SMEM((1, 2, 32), I32),
     nbrs_s=pltpu.SMEM((4, 6), I32),
     asked_s=pltpu.SMEM((4, 4, 6), I32),
@@ -40,7 +39,7 @@
     z_lhs=pltpu.VMEM((3, 256, 128), BF16),
     acc=pltpu.VMEM((4, 256, 128), F32),
     y_add=pltpu.VMEM((2, 4, 4, 8, 128), F32),
-    in_sems=pltpu.SemaphoreType.DMA((7,)),
+    in_sems=pltpu.SemaphoreType.DMA((6,)),
     list_send=pltpu.SemaphoreType.DMA((4,)),
     list_recv=pltpu.SemaphoreType.DMA((4,)),
     block_send=pltpu.SemaphoreType.DMA((2,)),
@@ -48,7 +47,7 @@
     face_send=pltpu.SemaphoreType.DMA((2, 4)),
     face_recv=pltpu.SemaphoreType.DMA((2, 4)),
 )
-OPERANDS = ("feat", "loads", "swaps", "nbrs", "occ", "wts", "gains", "out")
+OPERANDS = ("loads", "feat", "swaps", "nbrs", "occ", "wts", "gains", "out")
 
 
 def lanes_low():
@@ -379,7 +378,6 @@
         for i, (source, target) in enumerate(
             (
                 (r.feat, r.blocks),
-                (r.loads, r.loads_s),
                 (r.swaps, r.swaps_s),
                 (r.nbrs, r.nbrs_s),
                 (r.occ, r.occ_v),
@@ -410,9 +408,8 @@
     ]
     for_sides(lambda i: lists[i].start())
 
-    local[1].wait()
     local[0].wait()
-    load = r.loads_s[0]
+    load = r.loads[0]
     tail = jnp.maximum(load - 1, 0)
     r.outgoing[2] = r.blocks[jnp.where(odd, tail, 0)]
     partner = (grp, own + 1 - 2 * lax.rem(own, 2))
@@ -439,7 +436,7 @@
     )
     pair_copy.start()
 
-    for copy in local[2:]:
+    for copy in local[1:]:
         copy.wait()
     build_weights(r)
     places, final = settle_places(r, owners, own, odd, load, tail)
@@ -493,25 +490,25 @@
 
 
 def local_program(groups, owners, features, block_loads, swap_counts, neighbours, occupancy, conv_weights, norm_gains):
+    operands = (
+        features.reshape(4, 64, 512),
+        swap_counts,
+        neighbours,
+        occupancy,
+        conv_weights,
+        norm_gains,
+    )
     in_hbm = pl.BlockSpec(memory_space=pltpu.HBM)
     return pl.pallas_call(
         functools.partial(kernel, groups, owners),
         out_shape=jax.ShapeDtypeStruct((4, 8, 8, 512), BF16),
-        in_specs=[in_hbm] * 7,
+        in_specs=[pl.BlockSpec(memory_space=pltpu.SMEM)] + [in_hbm] * 6,
         out_specs=pl.BlockSpec(memory_space=pltpu.VMEM),
         scratch_shapes=list(SCRATCH.values()),
         compiler_params=pltpu.CompilerParams(
             collective_id=0, has_side_effects=True, vmem_limit_bytes=32 * 1024 * 1024
         ),
-    )(
-        features.reshape(4, 64, 512),
-        block_loads,
-        swap_counts,
-        neighbours,
-        occupancy,
-        conv_weights,
-        norm_gains,
-    )
+    )(block_loads, *[pltpu.with_memory_space_constraint(operand, pltpu.HBM) for operand in operands])
 
 
 def solution(mesh):

time: 25.5 us -> 21.3 us (0.84)
  local copies, waits for them, and re-layouts: 4.86 us -> 0.71 us
    unnamed x13 -> x1, local copies, waits for them, and re-layouts: 4.86 us -> 0.71 us
where the time goes in v4:
time: 21.3 us; the launch traced here: 21.2 us
  Pallas kernels  19.8 us (93%)
  local copies, waits for them, and re-layouts  0.71 us (3%)
  between operations  0.66 us (3%)
    pallas_call x1, Pallas kernels, local_program(): pl.pallas_call(functools.partial(kernel, groups, owners), out_shape=jax.S...  19.8 us
    unnamed x1, local copies, waits for them, and re-layouts  0.71 us

profile of v4, /device:TPU:119, one launch (start us, length us, event | category | flops | bytes accessed | tf_op | source)
XLA Modules:
  0.0 21.2 jit_solution(17756808916735093781)
XLA Ops:
  0.7 19.8 %shard_map.73 = bf16[4,8,8,512]{3,2,1,0:T(8,128)(2,1)S(1)} custom-call(s32[1]{0:T(128)S(6)} %copy.9.refs_0_, bf16[4,64,512]{2,1,0:T(8,128)(2,1)} %bitcast.1, s32[1,2,32]{2,1,0:T(2,128)} %refs_2_.1, s32[4,6]{1,0:T(4,128)} %refs_3_.1, s32[4,512]{1,0:T(4,128)} %refs_4_.1, bf16[2,27,64,64]{3,2,1,0:T(8,128)(2,1)} %refs_5_.1, f32[2,64]{1,0:T(2,128)} %refs_6_.1), custom_call_target="tpu_custom_call" | custom-call | tf_op jit(solution)/shard_map/pallas_call | solution.py:502
  20.4 0.7 %copy.10 = bf16[4,8,8,512]{3,2,1,0:T(8,128)(2,1)} copy(bf16[4,8,8,512]{3,2,1,0:T(8,128)(2,1)S(1)} %shard_map.73) | data formatting | bytes 524288

commit v5 on v4

--- a/solution.py
+++ b/solution.py
@@ -20,9 +20,7 @@
     swaps_s=pltpu.SMEM((1, 2, 32), I32),
     nbrs_s=pltpu.SMEM((4, 6), I32),
     asked_s=pltpu.SMEM((4, 4, 6), I32),
-    own_at=pltpu.SMEM((4, 6), I32),
-    far_at=pltpu.SMEM((4, 6), I32),
-    kind_at=pltpu.SMEM((4, 6), I32),
+    halo_at=pltpu.SMEM((4, 6), I32),
     occ_v=pltpu.VMEM((4, 512), I32),
     w_v=pltpu.VMEM((2, 27, 64, 64), BF16),
     g_v=pltpu.VMEM((2, 64), F32),
@@ -31,10 +29,10 @@
     nat=pltpu.VMEM((4, 256, 128), F32),
     faces=pltpu.VMEM((24, 32, 128), BF16),
     send_f=pltpu.VMEM((2, 16, 32, 128), BF16),
-    recv_first=pltpu.VMEM((16, 32, 128), BF16),
-    recv_second=pltpu.VMEM((16, 32, 128), BF16),
+    recv_first=pltpu.VMEM((41, 32, 128), BF16),
+    recv_second=pltpu.VMEM((41, 32, 128), BF16),
     lhs=pltpu.VMEM((3, 256, 640), BF16),
-    x_lhs=pltpu.VMEM((2, 3, 32, 640), BF16),
+    x_lhs=pltpu.VMEM((2, 32, 640), BF16),
     y_lhs=pltpu.VMEM((2, 32, 640), BF16),
     z_lhs=pltpu.VMEM((3, 256, 128), BF16),
     acc=pltpu.VMEM((4, 256, 128), F32),
@@ -129,40 +127,42 @@
     r.mask[...] = jnp.dot(strips, spread, preferred_element_type=F32)
 
 
-def rank_halos(r):
+def rank_halos(r, odd):
+    codes = (jnp.where(odd, 2, 1), jnp.where(odd, 1, 2), 3, 4)
+
     def rank_step(b, counts):
         counts = list(counts)
         for f in range(6):
             v = r.nbrs_s[b, f]
             s = lax.shift_right_arithmetic(v, 2)
-            rank = jnp.int32(0)
-            for i in range(4):
-                hit = s == i + 1
-                rank = jnp.where(hit, 4 * i + counts[i], rank)
-                counts[i] = counts[i] + hit.astype(I32)
-            r.kind_at[b, f] = s
-            r.own_at[b, f] = jnp.where(v >= 0, (v & 3) * 6 + (f ^ 1), 0)
-            r.far_at[b, f] = jnp.clip(rank, 0, 15)
+            at = jnp.where(s == 0, 16 + (v & 3) * 6 + (f ^ 1), 40)
+            for q in range(4):
+                hit = s == codes[q]
+                at = jnp.where(hit, 4 * q + jnp.minimum(counts[q], 3), at)
+                counts[q] = counts[q] + hit.astype(I32)
+            r.halo_at[b, f] = at
         return tuple(counts)
 
     lax.fori_loop(0, 4, rank_step, (jnp.int32(0),) * 4)
 
 
-def rank_asked(r):
+def rank_asked(r, odd, roles):
+    codes = (jnp.where(odd, 1, 2), jnp.where(odd, 2, 1), 4, 3)
+
     def ask_step(b, state):
         state = [list(row) for row in state]
         for f in range(6):
-            for i in range(4):
-                v = r.asked_s[i, b, f]
+            for i, q in enumerate(roles):
+                v = r.asked_s[q, b, f]
                 count = state[i][4]
-                hit = lax.shift_right_arithmetic(v, 2) == (i ^ 1) + 1
+                hit = lax.shift_right_arithmetic(v, 2) == codes[q]
                 face = (v & 3) * 6 + (f ^ 1)
                 for j in range(4):
                     state[i][j] = jnp.where(hit & (count == j), face, state[i][j])
                 state[i][4] = count + hit.astype(I32)
         return tuple(tuple(row) for row in state)
 
-    return lax.fori_loop(0, 4, ask_step, ((jnp.int32(0),) * 5,) * 4)
+    return lax.fori_loop(0, 4, ask_step, ((jnp.int32(0),) * 5,) * len(roles))
 
 
 def settle(r, places):
@@ -177,15 +177,21 @@
                 r.nat[t, rows, :] = kept[:, 128 * t : 128 * t + 128]
 
 
-def build_faces(r):
+def build_faces(r, recv_f):
     low = lanes_low()
+
+    def put(number, tiles):
+        face = jnp.concatenate(tiles, axis=0).astype(BF16)
+        r.faces[number] = face
+        recv_f[16 + number] = face
+
     for b in range(4):
         for f in range(2):
-            face = [r.nat[t, pl.ds(7 * f * 32 + b * 8, 8), :] for t in range(4)]
-            r.faces[b * 6 + f] = jnp.concatenate(face, axis=0).astype(BF16)
-            face = [r.nat[t, pl.ds(b * 8 + 7 * f, 8, stride=32), :] for t in range(4)]
-            r.faces[b * 6 + 2 + f] = jnp.concatenate(face, axis=0).astype(BF16)
-        for f in range(2):
+            put(b * 6 + f, [r.nat[t, pl.ds(7 * f * 32 + b * 8, 8), :] for t in range(4)])
+            put(
+                b * 6 + 2 + f,
+                [r.nat[t, pl.ds(b * 8 + 7 * f, 8, stride=32), :] for t in range(4)],
+            )
             face = []
             for x in range(4):
                 here = r.nat[3 * f, pl.ds(x * 32 + b * 8, 8), :]
@@ -195,22 +201,17 @@
                 else:
                     here = half_turn(here)
                 face.append(jnp.where(low, here, there))
-            r.faces[b * 6 + 4 + f] = jnp.concatenate(face, axis=0).astype(BF16)
-
-
-def pick_faces(r, layer, asked):
-    for i in range(4):
-        for j in range(4):
-            r.send_f[layer, 4 * i + j] = r.faces[asked[i][j]]
+            put(b * 6 + 4 + f, face)
+
+
+def pick_faces(r, layer, role, asked):
+    for j in range(4):
+        r.send_f[layer, 4 * role + j] = r.faces[asked[j]]
 
 
 def read_halos(r, recv_f):
     def halo(b, f):
-        kind = r.kind_at[b, f]
-        mine = r.faces[r.own_at[b, f]].astype(F32)
-        far = recv_f[r.far_at[b, f]].astype(F32)
-        zero = jnp.zeros((32, 128), F32)
-        both = jnp.where(kind == 0, mine, jnp.where(kind > 0, far, zero))
+        both = recv_f[r.halo_at[b, f]].astype(F32)
         return [both[8 * t : 8 * t + 8] for t in range(4)]
 
     return [[halo(b, f) for f in range(6)] for b in range(4)]
@@ -264,9 +265,7 @@
     for f in range(2):
         for pair in range(2):
             wide = [widen(halos[b][f], none8, none8) for b in (2 * pair, 2 * pair + 1)]
-            parts = [shifted_rows(tile) for tile in wide]
-            for dy in range(3):
-                put_pair(r.x_lhs, (f, dy), 16 * pair, [part[dy] for part in parts])
+            put_pair(r.x_lhs, (f,), 16 * pair, wide)
             wide = [widen(halos[b][2 + f], none8, none8) for b in (2 * pair, 2 * pair + 1)]
             put_pair(r.y_lhs, (f,), 16 * pair, wide)
     for pair in range(2):
@@ -280,20 +279,24 @@
             for dy in range(3):
                 put_pair(r.z_lhs, (dy,), x * 32 + 16 * pair, [part[dy] for part in parts[x]])
 
+    def over_rows(tile):
+        return (
+            shifted_rows(tile[:, 0:128])[0]
+            + tile[:, 128:256]
+            + shifted_rows(tile[:, 256:384])[2]
+        )
+
     for f in range(2):
-        window = jnp.concatenate(
-            [
-                jnp.concatenate([r.x_lhs[f, dy, :, pl.ds(128 * k, 256)] for dy in range(3)], axis=1)
-                for k in range(4)
-            ],
-            axis=0,
-        )
-        part = jnp.dot(
-            window, r.banded[layer, :, pl.ds(256 * f, 128)], preferred_element_type=F32
-        )
+        window = jnp.concatenate([r.x_lhs[f, :, pl.ds(128 * k, 256)] for k in range(4)], axis=0)
+        over_dy = jnp.concatenate(
+            [r.banded[layer, pl.ds(256 * dy, 256), pl.ds(256 * f, 128)] for dy in range(3)], axis=1
+        )
+        part = jnp.dot(window, over_dy, preferred_element_type=F32)
         for k in range(4):
-            rows = pl.ds(224 * f, 32)
-            r.acc[k, rows, :] = r.acc[k, rows, :] + part[32 * k : 32 * k + 32]
+            for b in range(4):
+                rows = pl.ds(224 * f + 8 * b, 8)
+                tile = part[32 * k + 8 * b : 32 * k + 8 * b + 8]
+                r.acc[k, rows, :] = r.acc[k, rows, :] + over_rows(tile)
 
         window = jnp.concatenate([r.y_lhs[f, :, pl.ds(128 * k, 256)] for k in range(4)], axis=0)
         part = jnp.dot(
@@ -302,11 +305,7 @@
         for k in range(4):
             for b in range(4):
                 tile = part[32 * k + 8 * b : 32 * k + 8 * b + 8]
-                r.y_add[f, k, b] = (
-                    shifted_rows(tile[:, 0:128])[0]
-                    + tile[:, 128:256]
-                    + shifted_rows(tile[:, 256:384])[2]
-                )
+                r.y_add[f, k, b] = over_rows(tile)
 
     window = jnp.concatenate([r.z_lhs[dy] for dy in range(3)], axis=1)
     ends = jnp.concatenate(
@@ -362,17 +361,38 @@
     own = lax.axis_index("curve")
     odd = lax.rem(own, 2) == 1
     sides = (
-        (grp, jnp.maximum(own - 1, 0)),
-        (grp, jnp.minimum(own + 1, owners - 1)),
+        (grp, jnp.clip(own - 1 + 2 * lax.rem(own, 2), 0, owners - 1)),
+        (grp, own + 1 - 2 * lax.rem(own, 2)),
         (jnp.maximum(grp - 1, 0), own),
         (jnp.minimum(grp + 1, groups - 1), own),
     )
-    there = (own > 0, own < owners - 1, grp > 0, grp < groups - 1)
-
-    def for_sides(step):
-        for i in range(4):
-            pl.when(there[i])(functools.partial(step, i))
-
+    there = ((own > 0) & (own < owners - 1), own >= 0, grp > 0, grp < groups - 1)
+    mirror = (0, 1, 3, 2)
+
+    def at_side(q, step):
+        if q == 1:
+            step()
+        else:
+            pl.when(there[q])(step)
+
+    def send(source, target, sems, q):
+        return pltpu.make_async_remote_copy(
+            src_ref=source,
+            dst_ref=target,
+            send_sem=sems[0],
+            recv_sem=sems[1],
+            device_id=sides[q],
+            device_id_type=MESH,
+        )
+
+    barrier = pltpu.get_barrier_semaphore()
+    for q in range(4):
+        at_side(
+            q,
+            lambda: pl.semaphore_signal(
+                barrier, inc=1, device_id=sides[q], device_id_type=MESH
+            ),
+        )
     local = [
         pltpu.make_async_copy(source, target, r.in_sems.at[i])
         for i, (source, target) in enumerate(
@@ -388,104 +408,97 @@
     ]
     for copy in local:
         copy.start()
-
-    barrier = pltpu.get_barrier_semaphore()
-    for_sides(
-        lambda i: pl.semaphore_signal(barrier, inc=1, device_id=sides[i], device_id_type=MESH)
-    )
-    pl.semaphore_wait(barrier, sum(flag.astype(I32) for flag in there))
-
-    lists = [
-        pltpu.make_async_remote_copy(
-            src_ref=r.nbrs,
-            dst_ref=r.asked_s.at[i ^ 1],
-            send_sem=r.list_send.at[i],
-            recv_sem=r.list_recv.at[i ^ 1],
-            device_id=sides[i],
-            device_id_type=MESH,
-        )
-        for i in range(4)
-    ]
-    for_sides(lambda i: lists[i].start())
-
-    local[0].wait()
     load = r.loads[0]
     tail = jnp.maximum(load - 1, 0)
+    local[0].wait()
     r.outgoing[2] = r.blocks[jnp.where(odd, tail, 0)]
-    partner = (grp, own + 1 - 2 * lax.rem(own, 2))
-    across = (grp, jnp.clip(own - 1 + 2 * lax.rem(own, 2), 0, owners - 1))
-    has_across = (own > 0) & (own < owners - 1)
-    cross_copy = pltpu.make_async_remote_copy(
-        src_ref=r.outgoing.at[pl.ds(2, 1)],
-        dst_ref=r.moved.at[pl.ds(2, 1)],
-        send_sem=r.block_send.at[0],
-        recv_sem=r.block_recv.at[0],
-        device_id=across,
-        device_id_type=MESH,
-    )
-    pl.when(has_across)(cross_copy.start)
     r.outgoing[0] = r.blocks[jnp.where(odd, 0, jnp.maximum(load - 2, 0))]
     r.outgoing[1] = r.blocks[jnp.where(odd, 1, tail)]
-    pair_copy = pltpu.make_async_remote_copy(
-        src_ref=r.outgoing.at[pl.ds(0, 2)],
-        dst_ref=r.moved.at[pl.ds(0, 2)],
-        send_sem=r.block_send.at[1],
-        recv_sem=r.block_recv.at[1],
-        device_id=partner,
-        device_id_type=MESH,
-    )
+    pl.semaphore_wait(barrier, sum(flag.astype(I32) for flag in there))
+
+    cross_copy = send(
+        r.outgoing.at[pl.ds(2, 1)],
+        r.moved.at[pl.ds(2, 1)],
+        (r.block_send.at[0], r.block_recv.at[0]),
+        0,
+    )
+    pair_copy = send(
+        r.outgoing.at[pl.ds(0, 2)],
+        r.moved.at[pl.ds(0, 2)],
+        (r.block_send.at[1], r.block_recv.at[1]),
+        1,
+    )
+    lists = [
+        send(
+            r.nbrs,
+            r.asked_s.at[mirror[q]],
+            (r.list_send.at[q], r.list_recv.at[mirror[q]]),
+            q,
+        )
+        for q in range(4)
+    ]
+    at_side(0, lists[0].start)
+    at_side(0, cross_copy.start)
+    for q in (2, 3, 1):
+        at_side(q, lists[q].start)
     pair_copy.start()
 
     for copy in local[1:]:
         copy.wait()
-    build_weights(r)
     places, final = settle_places(r, owners, own, odd, load, tail)
     build_mask(r, final)
-    rank_halos(r)
-    for i in range(4):
-
-        @pl.when(jnp.logical_not(there[i]))
+    build_weights(r)
+    rank_halos(r, odd)
+    for recv_f in (r.recv_first, r.recv_second):
+        recv_f[40] = jnp.zeros((32, 128), BF16)
+    for q in (0, 2, 3):
+
+        @pl.when(jnp.logical_not(there[q]))
         def _():
             for b in range(4):
                 for f in range(6):
-                    r.asked_s[i, b, f] = -1
-
-    for_sides(lambda i: lists[i ^ 1].wait_recv())
-    asked = rank_asked(r)
-
-    pl.when(has_across)(cross_copy.wait_recv)
+                    r.asked_s[q, b, f] = -1
+
+    for q in (1, 2, 3):
+        at_side(q, lists[mirror[q]].wait_recv)
+    asked = list(rank_asked(r, odd, (1, 2, 3)))
+    at_side(0, lists[0].wait_recv)
+    asked = list(rank_asked(r, odd, (0,))) + asked
+
     pair_copy.wait_recv()
+    at_side(0, cross_copy.wait_recv)
     settle(r, places)
 
     sent = []
     for layer in range(2):
         recv_f = (r.recv_first, r.recv_second)[layer]
-        build_faces(r)
-        pick_faces(r, layer, asked)
+        build_faces(r, recv_f)
         copies = [
-            pltpu.make_async_remote_copy(
-                src_ref=r.send_f.at[layer, pl.ds(4 * i, 4)],
-                dst_ref=recv_f.at[pl.ds(4 * (i ^ 1), 4)],
-                send_sem=r.face_send.at[layer, i],
-                recv_sem=r.face_recv.at[layer, i ^ 1],
-                device_id=sides[i],
-                device_id_type=MESH,
+            send(
+                r.send_f.at[layer, pl.ds(4 * q, 4)],
+                recv_f.at[pl.ds(4 * mirror[q], 4)],
+                (r.face_send.at[layer, q], r.face_recv.at[layer, mirror[q]]),
+                q,
             )
-            for i in range(4)
+            for q in range(4)
         ]
-        for_sides(lambda i: copies[i].start())
+        for q in (0, 2, 3, 1):
+            pick_faces(r, layer, q, asked[q])
+            at_side(q, copies[q].start)
 
         build_lhs(r)
         convolve_own(r, layer)
-        for_sides(lambda i: copies[i ^ 1].wait_recv())
+        for q in (1, 2, 3, 0):
+            at_side(q, copies[mirror[q]].wait_recv)
         add_halos(r, layer, read_halos(r, recv_f))
         finish(r, layer)
         sent += copies
 
-    for_sides(lambda i: lists[i].wait_send())
-    for_sides(lambda i: sent[i].wait_send())
-    for_sides(lambda i: sent[4 + i].wait_send())
-    pl.when(has_across)(cross_copy.wait_send)
+    for q in range(4):
+        at_side(q, lists[q].wait_send)
+        at_side(q, sent[q].wait_send)
+        at_side(q, sent[4 + q].wait_send)
+    at_side(0, cross_copy.wait_send)
     pair_copy.wait_send()
 
 

time: 21.3 us -> 20.6 us (0.967)
  Pallas kernels: 19.8 us -> 19 us
    pallas_call x1, Pallas kernels: 19.8 us -> 19 us  [local_program(): pl.pallas_call(functools.partial(kernel, groups, owners), out_shape=jax.S...]
where the time goes in v5:
time: 20.6 us; the launch traced here: 20.4 us
  Pallas kernels  19 us (92%)
  local copies, waits for them, and re-layouts  0.71 us (3%)
  between operations  0.66 us (3%)
    pallas_call x1, Pallas kernels, local_program(): pl.pallas_call(functools.partial(kernel, groups, owners), out_shape=jax.S...  19 us
    unnamed x1, local copies, waits for them, and re-layouts  0.71 us

profile of v5, /device:TPU:119, one launch (start us, length us, event | category | flops | bytes accessed | tf_op | source)
XLA Modules:
  0.0 20.4 jit_solution(14311909390335045632)
XLA Ops:
  0.7 19.0 %shard_map.73 = bf16[4,8,8,512]{3,2,1,0:T(8,128)(2,1)S(1)} custom-call(s32[1]{0:T(128)S(6)} %copy.9.refs_0_, bf16[4,64,512]{2,1,0:T(8,128)(2,1)} %bitcast.1, s32[1,2,32]{2,1,0:T(2,128)} %refs_2_.1, s32[4,6]{1,0:T(4,128)} %refs_3_.1, s32[4,512]{1,0:T(4,128)} %refs_4_.1, bf16[2,27,64,64]{3,2,1,0:T(8,128)(2,1)} %refs_5_.1, f32[2,64]{1,0:T(2,128)} %refs_6_.1), custom_call_target="tpu_custom_call" | custom-call | tf_op jit(solution)/shard_map/pallas_call | solution.py:515
  19.7 0.7 %copy.10 = bf16[4,8,8,512]{3,2,1,0:T(8,128)(2,1)} copy(bf16[4,8,8,512]{3,2,1,0:T(8,128)(2,1)S(1)} %shard_map.73) | data formatting | bytes 524288

commit v6 on v5

--- a/solution.py
+++ b/solution.py
@@ -15,7 +15,13 @@
 
 SCRATCH = dict(
     blocks=pltpu.VMEM((4, 64, 512), BF16),
-    moved=pltpu.VMEM((3, 64, 512), BF16),
+    moved=pltpu.VMEM((2, 64, 512), BF16),
+    crossed=pltpu.VMEM((1, 64, 512), BF16),
+    far_occ=pltpu.VMEM((4, 512), I32),
+    my_load=pltpu.VMEM((8, 128), I32),
+    far_load=pltpu.VMEM((8, 128), I32),
+    lent_f=pltpu.VMEM((6, 32, 128), BF16),
+    lent=pltpu.VMEM((4, 64, 128), F32),
     outgoing=pltpu.VMEM((3, 64, 512), BF16),
     swaps_s=pltpu.SMEM((1, 2, 32), I32),
     nbrs_s=pltpu.SMEM((4, 6), I32),
@@ -40,8 +46,8 @@
     in_sems=pltpu.SemaphoreType.DMA((6,)),
     list_send=pltpu.SemaphoreType.DMA((4,)),
     list_recv=pltpu.SemaphoreType.DMA((4,)),
-    block_send=pltpu.SemaphoreType.DMA((2,)),
-    block_recv=pltpu.SemaphoreType.DMA((2,)),
+    block_send=pltpu.SemaphoreType.DMA((4,)),
+    block_recv=pltpu.SemaphoreType.DMA((4,)),
     face_send=pltpu.SemaphoreType.DMA((2, 4)),
     face_recv=pltpu.SemaphoreType.DMA((2, 4)),
 )
@@ -68,7 +74,9 @@
 
 def build_weights(r):
     zero_w = jnp.zeros((64, 64), BF16)
-    for layer in range(2):
+
+    @pl.loop(0, 2)
+    def _(layer):
         for dx in range(3):
             for dy in range(3):
                 w = [r.w_v[layer, dx * 9 + dy * 3 + dz] for dz in range(3)]
@@ -106,17 +114,16 @@
     return places, final
 
 
-def build_mask(r, final):
-    block_no = lax.broadcasted_iota(I32, (4, 512), 0)
-    occupied = jnp.where((block_no < final) & (r.occ_v[...] > 0), 1.0, 0.0).astype(F32)
-    lane3 = lax.broadcasted_iota(I32, (4, 8, 128), 2)
-    sub3 = lax.broadcasted_iota(I32, (4, 8, 128), 1)
+def spread_rows(occupied):
+    blocks = occupied.shape[0]
+    lane3 = lax.broadcasted_iota(I32, (blocks, 8, 128), 2)
+    sub3 = lax.broadcasted_iota(I32, (blocks, 8, 128), 1)
     strips = []
     for x in range(8):
         strip = occupied[:, 128 * (x // 2) : 128 * (x // 2) + 128]
-        wide = jnp.broadcast_to(strip[:, None, :], (4, 8, 128))
+        wide = jnp.broadcast_to(strip[:, None, :], (blocks, 8, 128))
         pick = (lane3 // 8) == (sub3 + 8 * (x % 2))
-        strips.append(jnp.where(pick, wide, 0.0).reshape(32, 128))
+        strips.append(jnp.where(pick, wide, 0.0).reshape(8 * blocks, 128))
     strips = jnp.concatenate(strips, axis=0).astype(BF16)
     spread = jnp.where(
         lax.rem(lax.broadcasted_iota(I32, (128, 512), 0), 8)
@@ -124,7 +131,58 @@
         1.0,
         0.0,
     ).astype(BF16)
-    r.mask[...] = jnp.dot(strips, spread, preferred_element_type=F32)
+    return jnp.dot(strips, spread, preferred_element_type=F32)
+
+
+def build_mask(r, final):
+    block_no = lax.broadcasted_iota(I32, (4, 512), 0)
+    occupied = jnp.where((block_no < final) & (r.occ_v[...] > 0), 1.0, 0.0).astype(F32)
+    r.mask[...] = spread_rows(occupied)
+
+
+def lent_slot(r, owners, own, odd, rows):
+    flow_in = jnp.where(own > 0, r.swaps_s[0, 1, jnp.maximum(own - 1, 0)], 0)
+    flow_out = jnp.where(own < owners - 1, r.swaps_s[0, 1, own], 0)
+    pair_swap = r.swaps_s[0, 0, jnp.maximum(own - 2, 0)]
+    pair_flow = r.swaps_s[0, 1, jnp.maximum(own - 2, 0)]
+    appended = jnp.where(odd | (flow_in >= 0), 0, 1)
+    first = jnp.where(odd & (flow_out > 0), 0, -1)
+    far_load = r.far_load[pl.ds(0, rows), :]
+    return appended * (far_load + (pair_swap + pair_flow - flow_in)) + first
+
+
+def build_lent(r, slot):
+    low = lanes_low()
+    block_no = lax.broadcasted_iota(I32, (4, 128), 0)
+    kept = [
+        jnp.where((block_no == slot) & (r.far_occ[:, pl.ds(128 * t, 128)] > 0), 1.0, 0.0)
+        for t in range(4)
+    ]
+    keep = spread_rows(jnp.concatenate(kept, axis=1).astype(F32))
+    given = r.outgoing[2].astype(F32)
+    for x in range(8):
+        rows = [keep[32 * x + 8 * b : 32 * x + 8 * b + 8] for b in range(4)]
+        block = given[8 * x : 8 * x + 8]
+        block = jnp.where(rows[0] + rows[1] + rows[2] + rows[3] > 0.5, block, 0.0)
+        for t in range(4):
+            r.lent[t, pl.ds(8 * x, 8), :] = block[:, 128 * t : 128 * t + 128]
+
+    def put(number, tiles):
+        r.lent_f[number] = jnp.concatenate(tiles, axis=0).astype(BF16)
+
+    for f in range(2):
+        put(f, [r.lent[t, pl.ds(56 * f, 8), :] for t in range(4)])
+        put(2 + f, [r.lent[t, pl.ds(7 * f, 8, stride=8), :] for t in range(4)])
+        face = []
+        for x in range(4):
+            here = r.lent[3 * f, pl.ds(8 * x, 8), :]
+            there = r.lent[3 * f, pl.ds(8 * x + 32, 8), :]
+            if f == 0:
+                there = half_turn(there)
+            else:
+                here = half_turn(here)
+            face.append(jnp.where(low, here, there))
+        put(4 + f, face)
 
 
 def rank_halos(r, odd):
@@ -165,11 +223,13 @@
     return lax.fori_loop(0, 4, ask_step, ((jnp.int32(0),) * 5,) * len(roles))
 
 
-def settle(r, places):
+def settle(r, places, crossed):
     for j in range(4):
         mine = r.blocks[jnp.minimum(places[j], 3)].astype(F32)
-        other = r.moved[jnp.maximum(places[j] - 4, 0)].astype(F32)
+        other = r.moved[jnp.clip(places[j] - 4, 0, 1)].astype(F32)
         block = jnp.where(places[j] < 4, mine, other)
+        if crossed:
+            block = jnp.where(places[j] == 6, r.crossed[0].astype(F32), block)
         for x in range(8):
             rows = pl.ds(x * 32 + j * 8, 8)
             kept = jnp.where(r.mask[rows, :] > 0.5, block[8 * x : 8 * x + 8], 0.0)
@@ -185,17 +245,21 @@
         r.faces[number] = face
         recv_f[16 + number] = face
 
-    for b in range(4):
+    def tile(t, row):
+        return r.nat[t, pl.ds(pl.multiple_of(row, 8), 8), :]
+
+    @pl.loop(0, 4)
+    def _(b):
         for f in range(2):
-            put(b * 6 + f, [r.nat[t, pl.ds(7 * f * 32 + b * 8, 8), :] for t in range(4)])
+            put(b * 6 + f, [tile(t, 7 * f * 32 + b * 8) for t in range(4)])
             put(
                 b * 6 + 2 + f,
                 [r.nat[t, pl.ds(b * 8 + 7 * f, 8, stride=32), :] for t in range(4)],
             )
             face = []
             for x in range(4):
-                here = r.nat[3 * f, pl.ds(x * 32 + b * 8, 8), :]
-                there = r.nat[3 * f, pl.ds((x + 4) * 32 + b * 8, 8), :]
+                here = tile(3 * f, x * 32 + b * 8)
+                there = tile(3 * f, (x + 4) * 32 + b * 8)
                 if f == 0:
                     there = half_turn(there)
                 else:
@@ -209,10 +273,17 @@
         r.send_f[layer, 4 * role + j] = r.faces[asked[j]]
 
 
-def read_halos(r, recv_f):
+def read_halos(r, recv_f, odd, slot):
     def halo(b, f):
         both = recv_f[r.halo_at[b, f]].astype(F32)
-        return [both[8 * t : 8 * t + 8] for t in range(4)]
+        tiles = [both[8 * t : 8 * t + 8] for t in range(4)]
+        if slot is not None:
+            v = r.nbrs_s[b, f]
+            across = lax.shift_right_arithmetic(v, 2) == jnp.where(odd, 2, 1)
+            mine = slot == jnp.where(across, v & 3, -2)
+            lent = r.lent_f[f ^ 1].astype(F32)
+            tiles = [jnp.where(mine, lent[8 * t : 8 * t + 8], tiles[t]) for t in range(4)]
+        return tiles
 
     return [[halo(b, f) for f in range(6)] for b in range(4)]
 
@@ -232,13 +303,16 @@
 
 def build_lhs(r):
     none8 = jnp.zeros((8, 128), F32)
-    for x in range(8):
+
+    @pl.loop(0, 8)
+    def _(x):
         for pair in range(2):
-            row = x * 32 + pair * 16
             parts = []
             for b in (2 * pair, 2 * pair + 1):
-                tiles = [r.nat[t, pl.ds(x * 32 + b * 8, 8), :] for t in range(4)]
+                rows = pl.ds(pl.multiple_of(x * 32 + b * 8, 8), 8)
+                tiles = [r.nat[t, rows, :] for t in range(4)]
                 parts.append(shifted_rows(widen(tiles, none8, none8)))
+            row = pl.multiple_of(x * 32 + pair * 16, 16)
             for dy in range(3):
                 put_pair(r.lhs, (dy,), row, [part[dy] for part in parts])
 
@@ -331,20 +405,15 @@
 
 
 def finish(r, layer):
-    group_lane = lax.broadcasted_iota(I32, (256, 128), 1) // 64
-    group_row = lax.rem(lax.broadcasted_iota(I32, (256, 128), 0), 128) // 64
+    group_lane = lax.broadcasted_iota(I32, (128, 128), 1) // 64
+    group_row = lax.broadcasted_iota(I32, (128, 128), 0) // 64
     averager = jnp.where(group_lane == group_row, 1.0 / 64.0, 0.0).astype(BF16)
     gain = r.g_v[pl.ds(layer, 1), :]
     gain = jnp.concatenate([gain, gain], axis=1)
+    squares = jnp.concatenate([(r.acc[k] * r.acc[k]).astype(BF16) for k in range(4)], axis=0)
+    means = jnp.dot(squares, averager, preferred_element_type=F32)
     for k in range(4):
-        total = r.acc[k]
-        square = total * total
-        coarse = square.astype(BF16)
-        fine = (square - coarse.astype(F32)).astype(BF16)
-        mean = jnp.dot(
-            jnp.concatenate([coarse, fine], axis=1), averager, preferred_element_type=F32
-        )
-        scaled = total * lax.rsqrt(mean + 1e-5) * gain
+        scaled = r.acc[k] * lax.rsqrt(means[256 * k : 256 * k + 256] + 1e-5) * gain
         keep = r.mask[:, pl.ds(128 * k, 128)] > 0.5
         done = jnp.where(keep, jnp.maximum(scaled, 0.0), 0.0)
         if layer == 0:
@@ -410,6 +479,7 @@
         copy.start()
     load = r.loads[0]
     tail = jnp.maximum(load - 1, 0)
+    r.my_load[...] = jnp.zeros((8, 128), I32) + load
     local[0].wait()
     r.outgoing[2] = r.blocks[jnp.where(odd, tail, 0)]
     r.outgoing[0] = r.blocks[jnp.where(odd, 0, jnp.maximum(load - 2, 0))]
@@ -418,7 +488,7 @@
 
     cross_copy = send(
         r.outgoing.at[pl.ds(2, 1)],
-        r.moved.at[pl.ds(2, 1)],
+        r.crossed.at[pl.ds(0, 1)],
         (r.block_send.at[0], r.block_recv.at[0]),
         0,
     )
@@ -437,8 +507,19 @@
         )
         for q in range(4)
     ]
+    far = [
+        send(
+            source,
+            target,
+            (r.block_send.at[2 + i], r.block_recv.at[2 + i]),
+            0,
+        )
+        for i, (source, target) in enumerate(((r.my_load, r.far_load), (r.occ, r.far_occ)))
+    ]
     at_side(0, lists[0].start)
     at_side(0, cross_copy.start)
+    for copy in far:
+        at_side(0, copy.start)
     for q in (2, 3, 1):
         at_side(q, lists[q].start)
     pair_copy.start()
@@ -448,9 +529,14 @@
     places, final = settle_places(r, owners, own, odd, load, tail)
     build_mask(r, final)
     build_weights(r)
-    rank_halos(r, odd)
     for recv_f in (r.recv_first, r.recv_second):
         recv_f[40] = jnp.zeros((32, 128), BF16)
+
+    @pl.when(jnp.logical_not(there[0]))
+    def _():
+        r.far_load[...] = jnp.zeros((8, 128), I32)
+        r.far_occ[...] = jnp.zeros((4, 512), I32)
+
     for q in (0, 2, 3):
 
         @pl.when(jnp.logical_not(there[q]))
@@ -462,17 +548,16 @@
     for q in (1, 2, 3):
         at_side(q, lists[mirror[q]].wait_recv)
     asked = list(rank_asked(r, odd, (1, 2, 3)))
+
+    pair_copy.wait_recv()
+    settle(r, places, False)
+    build_faces(r, r.recv_first)
     at_side(0, lists[0].wait_recv)
     asked = list(rank_asked(r, odd, (0,))) + asked
-
-    pair_copy.wait_recv()
-    at_side(0, cross_copy.wait_recv)
-    settle(r, places)
 
     sent = []
     for layer in range(2):
         recv_f = (r.recv_first, r.recv_second)[layer]
-        build_faces(r, recv_f)
         copies = [
             send(
                 r.send_f.at[layer, pl.ds(4 * q, 4)],
@@ -482,15 +567,29 @@
             )
             for q in range(4)
         ]
-        for q in (0, 2, 3, 1):
+        if layer == 1:
+            build_faces(r, recv_f)
+        pick_faces(r, layer, 0, asked[0])
+        at_side(0, copies[0].start)
+        if layer == 0:
+            at_side(0, cross_copy.wait_recv)
+            settle(r, places, True)
+            build_faces(r, recv_f)
+        for q in (2, 3, 1):
             pick_faces(r, layer, q, asked[q])
             at_side(q, copies[q].start)
 
         build_lhs(r)
         convolve_own(r, layer)
+        if layer == 0:
+            for copy in far:
+                at_side(0, copy.wait_recv)
+            build_lent(r, lent_slot(r, owners, own, odd, 4))
+            rank_halos(r, odd)
         for q in (1, 2, 3, 0):
             at_side(q, copies[mirror[q]].wait_recv)
-        add_halos(r, layer, read_halos(r, recv_f))
+        slot = lent_slot(r, owners, own, odd, 8) if layer == 0 else None
+        add_halos(r, layer, read_halos(r, recv_f, odd, slot))
         finish(r, layer)
         sent += copies
 
@@ -498,7 +597,8 @@
         at_side(q, lists[q].wait_send)
         at_side(q, sent[q].wait_send)
         at_side(q, sent[4 + q].wait_send)
-    at_side(0, cross_copy.wait_send)
+    for copy in far + [cross_copy]:
+        at_side(0, copy.wait_send)
     pair_copy.wait_send()
 
 

time: 20.6 us -> 21.2 us (1.029)
  Pallas kernels: 19 us -> 19.4 us
    pallas_call x1, Pallas kernels: 19 us -> 19.4 us  [local_program(): pl.pallas_call(functools.partial(kernel, groups, owners), out_shape=jax.S...]
where the time goes in v6:
time: 21.2 us; the launch traced here: 20.8 us
  Pallas kernels  19.4 us (92%)
  local copies, waits for them, and re-layouts  0.71 us (3%)
  between operations  0.66 us (3%)
    pallas_call x1, Pallas kernels, local_program(): pl.pallas_call(functools.partial(kernel, groups, owners), out_shape=jax.S...  19.4 us
    unnamed x1, local copies, waits for them, and re-layouts  0.71 us

profile of v6, /device:TPU:119, one launch (start us, length us, event | category | flops | bytes accessed | tf_op | source)
XLA Modules:
  0.0 20.8 jit_solution(14674169852364032094)
XLA Ops:
  0.7 19.4 %shard_map.73 = bf16[4,8,8,512]{3,2,1,0:T(8,128)(2,1)S(1)} custom-call(s32[1]{0:T(128)S(6)} %copy.9.refs_0_, bf16[4,64,512]{2,1,0:T(8,128)(2,1)} %bitcast.1, s32[1,2,32]{2,1,0:T(2,128)} %refs_2_.1, s32[4,6]{1,0:T(4,128)} %refs_3_.1, s32[4,512]{1,0:T(4,128)} %refs_4_.1, bf16[2,27,64,64]{3,2,1,0:T(8,128)(2,1)} %refs_5_.1, f32[2,64]{1,0:T(2,128)} %refs_6_.1), custom_call_target="tpu_custom_call" | custom-call | tf_op jit(solution)/shard_map/pallas_call | solution.py:615
  20.1 0.7 %copy.10 = bf16[4,8,8,512]{3,2,1,0:T(8,128)(2,1)} copy(bf16[4,8,8,512]{3,2,1,0:T(8,128)(2,1)S(1)} %shard_map.73) | data formatting | bytes 524288

commit v7 on v5

--- a/solution.py
+++ b/solution.py
@@ -336,15 +336,15 @@
     averager = jnp.where(group_lane == group_row, 1.0 / 64.0, 0.0).astype(BF16)
     gain = r.g_v[pl.ds(layer, 1), :]
     gain = jnp.concatenate([gain, gain], axis=1)
+    parts = []
     for k in range(4):
-        total = r.acc[k]
-        square = total * total
+        square = r.acc[k] * r.acc[k]
         coarse = square.astype(BF16)
         fine = (square - coarse.astype(F32)).astype(BF16)
-        mean = jnp.dot(
-            jnp.concatenate([coarse, fine], axis=1), averager, preferred_element_type=F32
-        )
-        scaled = total * lax.rsqrt(mean + 1e-5) * gain
+        parts.append(jnp.concatenate([coarse, fine], axis=1))
+    means = jnp.dot(jnp.concatenate(parts, axis=0), averager, preferred_element_type=F32)
+    for k in range(4):
+        scaled = r.acc[k] * lax.rsqrt(means[256 * k : 256 * k + 256] + 1e-5) * gain
         keep = r.mask[:, pl.ds(128 * k, 128)] > 0.5
         done = jnp.where(keep, jnp.maximum(scaled, 0.0), 0.0)
         if layer == 0:

time: 20.6 us -> 20.7 us (level)
  no operation moved by 1% of the time
where the time goes in v7:
time: 20.7 us; the launch traced here: 20.5 us
  Pallas kernels  19.1 us (92%)
  local copies, waits for them, and re-layouts  0.71 us (3%)
  between operations  0.66 us (3%)
    pallas_call x1, Pallas kernels, local_program(): pl.pallas_call(functools.partial(kernel, groups, owners), out_shape=jax.S...  19.1 us
    unnamed x1, local copies, waits for them, and re-layouts  0.71 us

profile of v7, /device:TPU:119, one launch (start us, length us, event | category | flops | bytes accessed | tf_op | source)
XLA Modules:
  0.0 20.5 jit_solution(14181872911048929316)
XLA Ops:
  0.7 19.1 %shard_map.73 = bf16[4,8,8,512]{3,2,1,0:T(8,128)(2,1)S(1)} custom-call(s32[1]{0:T(128)S(6)} %copy.9.refs_0_, bf16[4,64,512]{2,1,0:T(8,128)(2,1)} %bitcast.1, s32[1,2,32]{2,1,0:T(2,128)} %refs_2_.1, s32[4,6]{1,0:T(4,128)} %refs_3_.1, s32[4,512]{1,0:T(4,128)} %refs_4_.1, bf16[2,27,64,64]{3,2,1,0:T(8,128)(2,1)} %refs_5_.1, f32[2,64]{1,0:T(2,128)} %refs_6_.1), custom_call_target="tpu_custom_call" | custom-call | tf_op jit(solution)/shard_map/pallas_call | solution.py:515
  19.8 0.7 %copy.10 = bf16[4,8,8,512]{3,2,1,0:T(8,128)(2,1)} copy(bf16[4,8,8,512]{3,2,1,0:T(8,128)(2,1)S(1)} %shard_map.73) | data formatting | bytes 524288

commit v8 on v7

--- a/solution.py
+++ b/solution.py
@@ -406,7 +406,7 @@
             )
         )
     ]
-    for copy in local:
+    for copy in local[:3]:
         copy.start()
     load = r.loads[0]
     tail = jnp.maximum(load - 1, 0)
@@ -442,6 +442,8 @@
     for q in (2, 3, 1):
         at_side(q, lists[q].start)
     pair_copy.start()
+    for copy in local[3:]:
+        copy.start()
 
     for copy in local[1:]:
         copy.wait()

time: 20.7 us -> 20.7 us (level)
  no operation moved by 1% of the time
where the time goes in v8:
time: 20.7 us; the launch traced here: 20.5 us
  Pallas kernels  19.1 us (92%)
  local copies, waits for them, and re-layouts  0.71 us (3%)
  between operations  0.66 us (3%)
    pallas_call x1, Pallas kernels, local_program(): pl.pallas_call(functools.partial(kernel, groups, owners), out_shape=jax.S...  19.1 us
    unnamed x1, local copies, waits for them, and re-layouts  0.71 us

profile of v8, /device:TPU:119, one launch (start us, length us, event | category | flops | bytes accessed | tf_op | source)
XLA Modules:
  0.0 20.5 jit_solution(2680618755944711830)
XLA Ops:
  0.7 19.1 %shard_map.73 = bf16[4,8,8,512]{3,2,1,0:T(8,128)(2,1)S(1)} custom-call(s32[1]{0:T(128)S(6)} %copy.9.refs_0_, bf16[4,64,512]{2,1,0:T(8,128)(2,1)} %bitcast.1, s32[1,2,32]{2,1,0:T(2,128)} %refs_2_.1, s32[4,6]{1,0:T(4,128)} %refs_3_.1, s32[4,512]{1,0:T(4,128)} %refs_4_.1, bf16[2,27,64,64]{3,2,1,0:T(8,128)(2,1)} %refs_5_.1, f32[2,64]{1,0:T(2,128)} %refs_6_.1), custom_call_target="tpu_custom_call" | custom-call | tf_op jit(solution)/shard_map/pallas_call | solution.py:517
  19.8 0.7 %copy.10 = bf16[4,8,8,512]{3,2,1,0:T(8,128)(2,1)} copy(bf16[4,8,8,512]{3,2,1,0:T(8,128)(2,1)S(1)} %shard_map.73) | data formatting | bytes 524288
